TPU v7x, 32 devices: a whole 2x2x4 slice. The times are simulated.
32 devices in a mesh: fsdp: 8 (over y, x, core), rep: 4 (over z).
Axes of the slice: x: 2, y: 2, z: 4, core: 2. Of those that a mesh axis runs over, the one named last changes fastest.
Arguments:
- tokens: bfloat16 [16384, 1024], P(('fsdp', 'rep')), may hold values from -6 to 6
- lengths: int32 [64], P(('fsdp', 'rep')), may hold values from 64 to 256, as said below
- cotangent: float32 [16384, 1024], P(('fsdp', 'rep')), may hold values from -6 to 6
- qkv_weight: bfloat16 [1024, 3072], P('fsdp'), may hold values from -0.1875 to 0.1875
- out_weight: bfloat16 [1024, 1024], P('fsdp'), may hold values from -0.75 to 0.75
- up_weight: bfloat16 [1024, 4096], P('fsdp'), may hold values from -0.1875 to 0.1875
- down_weight: bfloat16 [4096, 1024], P('fsdp'), may hold values from -0.09375 to 0.09375
- biases: bfloat16 [6, 1024], P(None, 'fsdp'), may hold values from -3 to 3
- up_bias: bfloat16 [4096], P('fsdp'), may hold values from -3 to 3
- gains: bfloat16 [2, 1024], P(None, 'fsdp'), may hold values from 0.5 to 1.5
Outputs:
- layer_out: bfloat16 [16384, 1024], P(('fsdp', 'rep'))
- token_grad: float32 [16384, 1024], P(('fsdp', 'rep'))
- qkv_grad: float32 [1024, 3072], P('fsdp')
- out_grad: float32 [1024, 1024], P('fsdp')
- up_grad: float32 [1024, 4096], P('fsdp')
- down_grad: float32 [4096, 1024], P('fsdp')
- biases_grad: float32 [6, 1024], P(None, 'fsdp')
- up_bias_grad: float32 [4096], P('fsdp')
- gains_grad: float32 [2, 1024], P(None, 'fsdp')
Inputs may be any that keep to these rules, and one draw needn't show every extreme that they name: lengths[s] is the number of live positions of sequence slot s; in every draw some slot holds 256 live positions and some holds 64.
All inputs are finite; a program needn't handle non-finite values.
Results may differ from a plain program's by a relative error of at most 0.017.
Values may be sent and summed in bfloat16 or wider, within the bound.
A program may use at most 192 MiB of HBM per device.

v0:
```python
import math

import jax
import jax.numpy as jnp
from jax import lax
from jax.sharding import PartitionSpec as P

H = 16


def for_sending(array):
    return jax.tree.map(lambda a: a.astype(jnp.bfloat16) if a.dtype == jnp.float32 else a, array)


def layer_norm(hidden, norm_gain, norm_shift):
    center = hidden - jnp.mean(hidden, axis=-1, keepdims=True)
    spread = jnp.mean(center * center, axis=-1, keepdims=True)
    return center * lax.rsqrt(spread + 1e-05) * norm_gain + norm_shift


def gelu_exact(values):
    return jax.nn.gelu(values, approximate=False)


def matmul(left_side, right_side):
    return jnp.dot(left_side, right_side, preferred_element_type=jnp.float32)


def transposed_left(left_side, right_side):
    return lax.dot_general(
        left_side, right_side, (((0,), (0,)), ((), ())), preferred_element_type=jnp.float32
    )


def transposed_right(left_side, right_side):
    return lax.dot_general(
        left_side, right_side, (((1,), (1,)), ((), ())), preferred_element_type=jnp.float32
    )


def column_sum(values):
    return jnp.sum(values.astype(jnp.float32), axis=0)


def one_slot(row_block, live_len, cot_block, full_weights):
    w_qkv, w_out, w_up, w_down, bias_low, bias_up_low, gain_low = full_weights
    bias_rows = bias_low.astype(jnp.float32)
    bias_up = bias_up_low.astype(jnp.float32)
    gain_rows = gain_low.astype(jnp.float32)
    model_width = w_qkv.shape[0]
    head_count = H
    head_size = model_width // head_count
    seq_len = row_block.shape[0]
    score_scale = 1.0 / math.sqrt(head_size)
    qkv_sums = matmul(row_block, w_qkv)
    query = (
        (qkv_sums[:, :model_width] + bias_rows[0])
        .astype(jnp.bfloat16)
        .reshape(seq_len, head_count, head_size)
    )
    key_heads = (
        qkv_sums[:, model_width : 2 * model_width]
        .astype(jnp.bfloat16)
        .reshape(seq_len, head_count, head_size)
    )
    value_heads = (
        (qkv_sums[:, 2 * model_width :] + bias_rows[1])
        .astype(jnp.bfloat16)
        .reshape(seq_len, head_count, head_size)
    )
    live_keys = jnp.arange(seq_len) < live_len
    scores = (
        jnp.einsum("shd,thd->hst", query, key_heads, preferred_element_type=jnp.float32)
        * score_scale
    )
    scores = jnp.where(live_keys[None, None, :], scores, -1e30)
    exp_scores = jnp.exp(scores - jnp.max(scores, axis=-1, keepdims=True))
    attn_probs = exp_scores / jnp.sum(exp_scores, axis=-1, keepdims=True)
    probs_low = attn_probs.astype(jnp.bfloat16)
    mixed = jnp.einsum("hst,thd->shd", probs_low, value_heads, preferred_element_type=jnp.float32)
    mixed = mixed.reshape(seq_len, model_width).astype(jnp.bfloat16)
    residual = row_block.astype(jnp.float32) + matmul(mixed, w_out) + bias_rows[2]
    first_norm, first_pull = jax.vjp(layer_norm, residual, gain_rows[0], bias_rows[3])
    first_low = first_norm.astype(jnp.bfloat16)
    inner_sums = matmul(first_low, w_up) + bias_up
    act_value, act_pull = jax.vjp(gelu_exact, inner_sums)
    act_low = act_value.astype(jnp.bfloat16)
    branch = matmul(act_low, w_down) + bias_rows[4]
    final_norm, final_pull = jax.vjp(layer_norm, first_norm + branch, gain_rows[1], bias_rows[5])
    grad_out = cot_block * live_keys[:, None].astype(jnp.float32)
    grad_h2, grad_gain_two, grad_shift_two = final_pull(grad_out)
    grad_branch = grad_h2.astype(jnp.bfloat16)
    grad_down = transposed_left(act_low, grad_branch)
    (grad_inner_wide,) = act_pull(transposed_right(grad_branch, w_down))
    grad_inner = grad_inner_wide.astype(jnp.bfloat16)
    grad_up = transposed_left(first_low, grad_inner)
    grad_first = grad_h2 + transposed_right(grad_inner, w_up)
    grad_h1, grad_gain_one, grad_shift_one = first_pull(grad_first)
    grad_attn = grad_h1.astype(jnp.bfloat16)
    grad_outw = transposed_left(mixed, grad_attn)
    grad_mixed = (
        transposed_right(grad_attn, w_out)
        .astype(jnp.bfloat16)
        .reshape(seq_len, head_count, head_size)
    )
    grad_probs = jnp.einsum(
        "shd,thd->hst", grad_mixed, value_heads, preferred_element_type=jnp.float32
    )
    shared = jnp.sum(attn_probs * grad_probs, axis=-1, keepdims=True)
    grad_scores = (attn_probs * (grad_probs - shared)).astype(jnp.bfloat16)
    grad_query = (
        jnp.einsum("hst,thd->shd", grad_scores, key_heads, preferred_element_type=jnp.float32)
        * score_scale
    )
    grad_query = grad_query.astype(jnp.bfloat16).reshape(seq_len, model_width)
    grad_key = (
        jnp.einsum("hst,shd->thd", grad_scores, query, preferred_element_type=jnp.float32)
        * score_scale
    )
    grad_key = grad_key.astype(jnp.bfloat16).reshape(seq_len, model_width)
    grad_value = jnp.einsum(
        "hst,shd->thd", probs_low, grad_mixed, preferred_element_type=jnp.float32
    )
    grad_value = grad_value.astype(jnp.bfloat16).reshape(seq_len, model_width)
    grad_qkv = jnp.concatenate([grad_query, grad_key, grad_value], axis=1)
    grad_qkvw = transposed_left(row_block, grad_qkv)
    grad_rows = grad_h1 + transposed_right(grad_qkv, w_qkv)
    grad_biases = jnp.stack(
        [
            column_sum(grad_query),
            column_sum(grad_value),
            column_sum(grad_attn),
            grad_shift_one,
            column_sum(grad_branch),
            grad_shift_two,
        ]
    )
    grad_gains = jnp.stack([grad_gain_one, grad_gain_two])
    local_grads = (
        grad_qkvw,
        grad_outw,
        grad_up,
        grad_down,
        grad_biases,
        column_sum(grad_inner),
        grad_gains,
    )
    return (final_norm.astype(jnp.bfloat16), grad_rows, local_grads)


def local(
    tokens,
    lengths,
    cotangent,
    qkv_weight,
    out_weight,
    up_weight,
    down_weight,
    biases,
    up_bias,
    gains,
):
    shards = (qkv_weight, out_weight, up_weight, down_weight, biases, up_bias, gains)
    slot_count = lengths.shape[0]
    seq_len = tokens.shape[0] // slot_count
    outputs = []
    token_grads = []
    totals = None
    for slot_index in range(slot_count):
        full_weights = (
            lax.all_gather(shards[0], "fsdp", axis=0, tiled=True),
            lax.all_gather(shards[1], "fsdp", axis=0, tiled=True),
            lax.all_gather(shards[2], "fsdp", axis=0, tiled=True),
            lax.all_gather(shards[3], "fsdp", axis=0, tiled=True),
            lax.all_gather(shards[4], "fsdp", axis=1, tiled=True),
            lax.all_gather(shards[5], "fsdp", axis=0, tiled=True),
            lax.all_gather(shards[6], "fsdp", axis=1, tiled=True),
        )
        row_block = tokens[slot_index * seq_len : (slot_index + 1) * seq_len]
        cot_block = cotangent[slot_index * seq_len : (slot_index + 1) * seq_len]
        layer_rows, grad_rows, local_grads = one_slot(
            row_block, lengths[slot_index], cot_block, full_weights
        )
        outputs.append(layer_rows)
        token_grads.append(grad_rows)
        totals = local_grads if totals is None else jax.tree.map(jnp.add, totals, local_grads)
    totals = (
        lax.psum_scatter(totals[0], "fsdp", scatter_dimension=0, tiled=True),
        lax.psum_scatter(totals[1], "fsdp", scatter_dimension=0, tiled=True),
        lax.psum_scatter(totals[2], "fsdp", scatter_dimension=0, tiled=True),
        lax.psum_scatter(totals[3], "fsdp", scatter_dimension=0, tiled=True),
        lax.psum_scatter(totals[4], "fsdp", scatter_dimension=1, tiled=True),
        lax.psum_scatter(totals[5], "fsdp", scatter_dimension=0, tiled=True),
        lax.psum_scatter(totals[6], "fsdp", scatter_dimension=1, tiled=True),
    )
    summed = jax.tree.map(
        lambda part: part.astype(jnp.float32), lax.psum(for_sending(totals), "rep")
    )
    return (
        jnp.concatenate(outputs, axis=0),
        jnp.concatenate(token_grads, axis=0),
        summed[0],
        summed[1],
        summed[2],
        summed[3],
        summed[4],
        summed[5],
        summed[6],
    )


def solution(mesh):
    in_specs = (
        P(("fsdp", "rep"), None),
        P(("fsdp", "rep")),
        P(("fsdp", "rep"), None),
        P("fsdp", None),
        P("fsdp", None),
        P("fsdp", None),
        P("fsdp", None),
        P(None, "fsdp"),
        P("fsdp"),
        P(None, "fsdp"),
    )
    out_specs = (
        P(("fsdp", "rep"), None),
        P(("fsdp", "rep"), None),
        P("fsdp", None),
        P("fsdp", None),
        P("fsdp", None),
        P("fsdp", None),
        P(None, "fsdp"),
        P("fsdp"),
        P(None, "fsdp"),
    )
    return jax.shard_map(local, mesh=mesh, in_specs=in_specs, out_specs=out_specs, check_vma=False)
```

profile of v0, /device:TPU:0, one launch (start us, length us, event | category | flops | bytes accessed | tf_op | source)
XLA Modules:
  0.0 887.6 jit_solution(17587757289119557393)
XLA Ops:
  10.7 10.3 %all-gather = bf16[8,1,512]{2,1,0:T(2,128)(2,1)S(1)} all-gather(bf16[1,1,512]{2,1,0:T(2,128)(2,1)S(1)} %reshape.257), channel_id=1, replica_groups=mesh['fsdp'=8,'rep'=4] {'fsdp'}, dimensions={0}, use_global_device_ids=true | all-gather | bytes 9216 | tf_op jit(solution)/shard_map/all_gather | solution.py:176
  21.7 8.7 all_gather.31
  30.4 8.0 all_gather.29
  44.6 13.6 %all-gather.6.cloned.1.call-done = bf16[1024,3072]{1,0:T(8,128)(2,1)} async-done(((bf16[128,3072]{1,0:T(8,128)(2,1)}), bf16[1024,3072]{1,0:T(8,128)(2,1)}) %all-gather.6.cloned.1.call-update) | async-done | bytes 6291472 | tf_op jit(solution)/shard_map/all_gather | solution.py:171
  100.3 44.0 %all-gather.10.cloned.1.call-done = bf16[1024,4096]{1,0:T(8,128)(2,1)} async-done(((bf16[128,4096]{1,0:T(8,128)(2,1)}), bf16[1024,4096]{1,0:T(8,128)(2,1)}) %all-gather.10.cloned.1.call-update) | async-done | bytes 8388624 | tf_op jit(solution)/shard_map/all_gather | solution.py:173
  144.3 16.2 %multiply_convert_fusion.2 = (bf16[256,4096]{1,0:T(8,128)(2,1)}, f32[256,4096]{1,0:T(8,128)}, f32[256,4096]{1,0:T(8,128)}) fusion(f32[4096]{0:T(1024)S(1)} %bitcast.187, bf16[1024,4096]{1,0:T(8,128)(2,1)} %all-gather.10.cloned.1.call-done, f32[256,1024]{1,0:T(8,128)S(1)} %get-tuple-element.116, f32[256]{0:T(256)S(1)} %fusion.55, ...), kind=kOutput, calls=%fused_computation.19 | convolution fusion | flops 2218000384 | bytes 19949568 | tf_op jit(solution)/shard_map/dot_general | solution.py:26
  160.5 39.9 %all-gather.12.cloned.1.call-done = bf16[4096,1024]{1,0:T(8,128)(2,1)} async-done(((bf16[512,1024]{1,0:T(8,128)(2,1)}), bf16[4096,1024]{1,0:T(8,128)(2,1)}) %all-gather.12.cloned.1.call-update) | async-done | bytes 8388624 | tf_op jit(solution)/shard_map/all_gather | solution.py:174
  200.5 6.6 fusion.86
  207.4 16.7 %multiply_convert_fusion.3 = (bf16[256,4096]{1,0:T(8,128)(2,1)S(1)}, f32[256,4096]{1,0:T(8,128)}, f32[256,4096]{1,0:T(8,128)}) fusion(f32[4096]{0:T(1024)S(1)} %bitcast.188, bf16[1024,4096]{1,0:T(8,128)(2,1)S(1)} %copy-done.73, f32[256,1024]{1,0:T(8,128)S(1)} %get-tuple-element.109, f32[1024]{0:T(1024)S(1)} %bitcast.167, f32[1024]{0:T(1024)S(1)} %bitcast.147, ...), kind=kOutput, calls=%fused_computation.34 | convolution fusion | flops 2218000384 | bytes 19949568 | tf_op jit(solution)/shard_map/dot_general | solution.py:26
  232.0 11.8 %convert_reduce_fusion = (f32[4096]{0:T(1024)}, bf16[256,4096]{1,0:T(8,128)(2,1)S(1)}) fusion(f32[256,4096]{1,0:T(8,128)S(1)} %copy-done.77, f32[256,4096]{1,0:T(8,128)} %get-tuple-element.117, bf16[256,1024]{1,0:T(8,128)(2,1)S(1)} %get-tuple-element.62, bf16[4096,1024]{1,0:T(8,128)(2,1)} %all-gather.12.cloned.1.call-done), kind=kOutput, calls=%fused_computation.11 | convolution fusion | flops 2164256768 | bytes 19415040 | tf_op jit(solution)/shard_map/dot_general | solution.py:36
  243.8 6.8 convolution_add_fusion.9
  250.7 11.8 %convert_reduce_fusion.1 = (f32[4096]{0:T(1024)}, bf16[256,4096]{1,0:T(8,128)(2,1)S(1)}) fusion(f32[256,4096]{1,0:T(8,128)S(1)} %copy-done.78, f32[256,4096]{1,0:T(8,128)} %get-tuple-element.110, bf16[256,1024]{1,0:T(8,128)(2,1)S(1)} %get-tuple-element.66, bf16[4096,1024]{1,0:T(8,128)(2,1)} %all-gather.12.cloned.1.call-done), kind=kOutput, calls=%fused_computation.12 | convolution fusion | flops 2164256768 | bytes 19415040 | tf_op jit(solution)/shard_map/dot_general | solution.py:36
  262.5 7.8 multiply_reduce_fusion.5
  279.2 5.2 multiply_reduce_fusion.1
  309.9 6.4 add_bitcast_fusion
  320.6 10.1 %convolution_add_fusion = f32[4096,1024]{1,0:T(8,128)} fusion(f32[4096,1024]{1,0:T(8,128)S(1)} %fusion.88, bf16[256,4096]{1,0:T(8,128)(2,1)} %get-tuple-element.79, bf16[256,1024]{1,0:T(8,128)(2,1)} %copy-done.30), kind=kOutput, calls=%fused_computation.3 | convolution fusion | flops 2151677952 | bytes 36175872 | tf_op jit(solution)/shard_map/dot_general | solution.py:30
  335.0 10.1 %convolution_add_fusion.1 = f32[1024,4096]{1,0:T(8,128)} fusion(f32[1024,4096]{1,0:T(8,128)S(1)} %fusion.69, bf16[256,4096]{1,0:T(8,128)(2,1)} %copy-done.16, f32[256,1024]{1,0:T(8,128)S(1)} %get-tuple-element.116, f32[256]{0:T(256)} %copy-done.59, f32[256]{0:T(256)S(1)} %broadcast_multiply_fusion.1, f32[1024]{0:T(1024)S(1)} %bitcast.170, f32[1024]{0:T(1024)S(1)} %bitcast.152), kind=kOutput, calls=%fused_computation.4 | convolution fusion | flops 2152988672 | bytes 36710400 | tf_op jit(solution)/shard_map/dot_general | solution.py:30
  350.0 85.5 %reduce-scatter.9.cloned.1.call-done = f32[128,3072]{0,1:T(8,128)} async-done(((f32[1024,3072]{0,1:T(8,128)}), f32[128,3072]{0,1:T(8,128)}) %reduce-scatter.9.cloned.1.call-update) | async-done | bytes 1572880 | tf_op jit(solution)/shard_map/reduce_scatter | solution.py:188
  438.0 117.6 %reduce-scatter.15.cloned.1.call-done = f32[512,1024]{1,0:T(8,128)} async-done(((f32[4096,1024]{1,0:T(8,128)}), f32[512,1024]{1,0:T(8,128)}) %reduce-scatter.15.cloned.1.call-update) | async-done | bytes 2097168 | tf_op jit(solution)/shard_map/reduce_scatter | solution.py:191
  558.3 117.2 %reduce-scatter.13.cloned.1.call-done = f32[128,4096]{1,0:T(8,128)} async-done(((f32[1024,4096]{1,0:T(8,128)}), f32[128,4096]{1,0:T(8,128)}) %reduce-scatter.13.cloned.1.call-update) | async-done | bytes 2097168 | tf_op jit(solution)/shard_map/reduce_scatter | solution.py:190
  679.5 23.5 %all-reduce = bf16[4096]{0:T(1024)(128)(2,1)S(1)} all-reduce(f32[4096]{0:T(1024)S(1)} %add.271), channel_id=7, replica_groups=mesh['fsdp'=8,'rep'=4] {'fsdp'}, use_global_device_ids=true, to_apply=%region_46.47.clone | all-reduce | flops 4096 | bytes 24576
  717.2 29.9 %reduce-scatter.17.cloned.1.call-done = f32[6,128]{1,0:T(8,128)} async-done(((f32[6,1024]{1,0:T(8,128)}), f32[6,128]{1,0:T(8,128)}) %reduce-scatter.17.cloned.1.call-update) | async-done | bytes 3088 | tf_op jit(solution)/shard_map/reduce_scatter | solution.py:192
  747.8 11.8 %all-reduce.1 = (bf16[6,128]{1,0:T(8,128)(2,1)S(1)}, bf16[512]{0:T(512)(128)(2,1)S(1)}, bf16[2,128]{1,0:T(2,128)(2,1)S(1)}) all-reduce(bf16[6,128]{1,0:T(8,128)(2,1)S(1)} %convert_element_type.295, bf16[512]{0:T(512)(128)(2,1)S(1)} %dynamic-slice.3, bf16[2,128]{1,0:T(2,128)(2,1)S(1)} %copy.87), channel_id=1, replica_groups=mesh['fsdp'=8,'rep'=4] {'rep'}, use_global_device_ids=true, to_apply=%region_43.44 | all-reduce | flops 1536 | bytes 6144 | tf_op jit(solution)/shard_map/psum | solution.py:197
  761.4 111.3 %all-reduce.5.cloned.1.call-done = (bf16[128,3072]{0,1:T(8,128)(2,1)}, bf16[128,1024]{1,0:T(8,128)(2,1)}, bf16[128,4096]{1,0:T(8,128)(2,1)}, bf16[512,1024]{1,0:T(8,128)(2,1)}) async-done(((bf16[128,3072]{0,1:T(8,128)(2,1)}, bf16[128,1024]{1,0:T(8,128)(2,1)}, bf16[128,4096]{1,0:T(8,128)(2,1)}, bf16[512,1024]{1,0:T(8,128)(2,1)}), (bf16[128,3072]{0,1:T(8,128)(2,1)}, bf16[128,1024]{1,0:T(8,128)(2,1)}, ...) | async-done | bytes 3145744 | tf_op jit(solution)/shard_map/psum | solution.py:197
  (288 shorter events, 140.7 us)
Async XLA Ops:
  7.2 51.0 %all-gather.6.cloned.1.call-start = ((), (), s32[]{:S(2)}) async-start(), calls=%async_computation.6 | async-start | bytes 7077888 | tf_op jit(solution)/shard_map/all_gather | solution.py:171
  7.9 80.1 %all-gather.8.cloned.1.call-start = ((), (), s32[]{:S(2)}) async-start(), calls=%async_computation.7 | async-start | bytes 2359296 | tf_op jit(solution)/shard_map/all_gather | solution.py:172
  8.7 135.6 %all-gather.10.cloned.1.call-start = ((), (), s32[]{:S(2)}) async-start(), calls=%async_computation.8 | async-start | bytes 9437184 | tf_op jit(solution)/shard_map/all_gather | solution.py:173
  9.4 191.1 %all-gather.12.cloned.1.call-start = ((), (), s32[]{:S(2)}) async-start(), calls=%async_computation.9 | async-start | bytes 9437184 | tf_op jit(solution)/shard_map/all_gather | solution.py:174
  10.0 338.1 %reduce-scatter.11.cloned.1.call-start = ((), (), s32[]{:S(2)}) async-start(), calls=%async_computation.11 | async-start | bytes 4718592 | tf_op jit(solution)/shard_map/reduce_scatter | solution.py:189
  98.7 45.6 %copy-start.58 = (f32[8,1,512]{2,1,0:T(1,128)S(1)}, f32[8,1,512]{2,1,0:T(1,128)}, u32[]{:S(2)}) copy-start(f32[8,1,512]{2,1,0:T(1,128)} %convert_element_type.303) | copy-start | bytes 49156
  100.3 170.0 %copy-start.59 = (f32[256]{0:T(256)}, f32[256]{0:T(256)S(1)}, u32[]{:S(2)}) copy-start(f32[256]{0:T(256)S(1)} %fusion.55) | copy-start | bytes 3076
  100.3 170.0 %copy-start.44 = (f32[256]{0:T(256)}, f32[256]{0:T(256)S(1)}, u32[]{:S(2)}) copy-start(f32[256]{0:T(256)S(1)} %fusion.53) | copy-start | bytes 3076
  144.3 56.2 %copy-start.66 = (f32[1,1024]{1,0:T(1,128)S(1)}, f32[1,1024]{1,0:T(1,128)}, u32[]{:S(2)}) copy-start(f32[1,1024]{1,0:T(1,128)} %get-tuple-element.90) | copy-start | bytes 12292
  200.5 23.6 %slice-start = ((s8[8388608]{0:T(1024)(128)(4,1)}), s8[4194304]{0:T(1024)(128)(4,1)S(1)}, s32[]{:S(2)}) async-start(s8[8388608]{0:T(1024)(128)(4,1)} %bitcast.195), calls=%async_computation.17 | async-start | bytes 8388608
  287.9 147.7 %reduce-scatter.9.cloned.1.call-start = ((), (), s32[]{:S(2)}) async-start(), calls=%async_computation.10 | async-start | bytes 14155776 | tf_op jit(solution)/shard_map/reduce_scatter | solution.py:188
  316.3 239.3 %reduce-scatter.15.cloned.1.call-start = ((), (), s32[]{:S(2)}) async-start(), calls=%async_computation.13 | async-start | bytes 18874368 | tf_op jit(solution)/shard_map/reduce_scatter | solution.py:191
  330.7 344.7 %reduce-scatter.13.cloned.1.call-start = ((), (), s32[]{:S(2)}) async-start(), calls=%async_computation.12 | async-start | bytes 18874368 | tf_op jit(solution)/shard_map/reduce_scatter | solution.py:190
  345.2 371.1 %reduce-scatter.19.cloned.1.call-start = ((), (), s32[]{:S(2)}) async-start(), calls=%async_computation.15 | async-start | bytes 589824
  346.8 400.3 %reduce-scatter.17.cloned.1.call-start = ((), (), s32[]{:S(2)}) async-start(), calls=%async_computation.14 | async-start | bytes 36864 | tf_op jit(solution)/shard_map/reduce_scatter | solution.py:192
  348.0 524.7 %all-reduce.5.cloned.1.call-start = ((), (), s32[]{:S(2)}) async-start(), calls=%async_computation.16 | async-start | bytes 6291456 | tf_op jit(solution)/shard_map/psum | solution.py:197
  437.9 240.3 %copy-start.75 = (u32[32]{0:T(128)S(1)}, u32[32]{0:T(128)}, u32[]{:S(2)}) copy-start(u32[32]{0:T(128)} %constant.95) | copy-start | bytes 388
  437.9 241.5 %copy-start.56 = (f32[4096]{0:T(1024)S(1)}, f32[4096]{0:T(1024)}, u32[]{:S(2)}) copy-start(f32[4096]{0:T(1024)} %get-tuple-element.57) | copy-start | bytes 49156
  437.9 241.5 %copy-start.57 = (f32[4096]{0:T(1024)S(1)}, f32[4096]{0:T(1024)}, u32[]{:S(2)}) copy-start(f32[4096]{0:T(1024)} %get-tuple-element.59) | copy-start | bytes 49156
  438.0 265.1 %copy-start.28 = (bf16[256,1024]{1,0:T(8,128)(2,1)S(1)}, bf16[256,1024]{1,0:T(8,128)(2,1)}, u32[]{:S(2)}) copy-start(bf16[256,1024]{1,0:T(8,128)(2,1)} %get-tuple-element.87) | copy-start | bytes 1572868
  558.3 146.8 %copy-start.12 = (f32[256,1024]{1,0:T(8,128)S(1)}, f32[256,1024]{1,0:T(8,128)}, u32[]{:S(2)}) copy-start(f32[256,1024]{1,0:T(8,128)} %copy-done.11) | copy-start | bytes 3145732
  558.3 146.8 %copy-start.18 = (bf16[16,64,256]{2,1,0:T(8,128)(2,1)S(1)}, bf16[16,64,256]{2,1,0:T(8,128)(2,1)}, u32[]{:S(2)}) copy-start(bf16[16,64,256]{2,1,0:T(8,128)(2,1)} %copy-done.17) | copy-start | bytes 1572868
  558.3 146.8 %copy-start.20 = (bf16[16,64,256]{2,1,0:T(8,128)(2,1)S(1)}, bf16[16,64,256]{2,1,0:T(8,128)(2,1)}, u32[]{:S(2)}) copy-start(bf16[16,64,256]{2,1,0:T(8,128)(2,1)} %copy-done.19) | copy-start | bytes 1572868
  558.3 146.8 %copy-start.72 = (f32[256]{0:T(256)S(1)}, f32[256]{0:T(256)}, u32[]{:S(2)}) copy-start(f32[256]{0:T(256)} %copy-done.71) | copy-start | bytes 3076
  (68 other events, 321.0 us)
Sparse Core Ops, SparseCore 0:
  9.9 48.2 all-gather.5
  60.0 27.8 all-gather.7
  89.9 54.3 all-gather.9
  146.0 54.3 all-gather.11
  288.0 51.3 reduce-scatter.10
  343.1 92.3 reduce-scatter.8
  439.6 115.9 reduce-scatter.14
  559.5 115.9 reduce-scatter.12
  678.9 34.1 reduce-scatter.18
  715.9 31.2 reduce-scatter.16
  750.5 122.1 all-reduce.4
where the time goes:
time: 897 us; the launch traced here: 888 us
  waiting for transfers between devices  566 us (63%)
  matrix products  174 us (19%)
  blocking collectives  62.4 us (7%)
  other arithmetic  43.5 us (5%)
  local copies, waits for them, and re-layouts  24.5 us (3%)
  between operations  15.9 us (2%)
    reduce_scatter x1, waiting for transfers between devices, local(): lax.psum_scatter(totals[3], 'fsdp', scatter_dimension=0, tiled=True)  118 us
    reduce_scatter x1, waiting for transfers between devices, local(): lax.psum_scatter(totals[2], 'fsdp', scatter_dimension=0, tiled=True)  117 us
    psum x1, waiting for transfers between devices, local(): lax.psum(for_sending(totals), 'rep')  111 us
    reduce_scatter x1, waiting for transfers between devices, local(): lax.psum_scatter(totals[0], 'fsdp', scatter_dimension=0, tiled=True)  85.5 us
    dot_general x8, matrix products, transposed_right(): lax.dot_general(left_side, right_side, (((1,), (1,)), ((), ())), preferre...  52.5 us
    dot_general x8, matrix products, matmul(): return jnp.dot(left_side, right_side, preferred_element_type=jnp.float32)  52.1 us
    all_gather x1, waiting for transfers between devices, local(): lax.all_gather(shards[2], 'fsdp', axis=0, tiled=True)  44 us
    dot_general x8, matrix products, transposed_left(): lax.dot_general(left_side, right_side, (((0,), (0,)), ((), ())), preferre...  41.9 us
  transfers between devices with their start and end apart: 11, of which 9 were waited for; matrix products, arithmetic and copies ran while one was open for 16% of the time, Pallas kernels for 0%

commit v1 on v0

v1 whole, which is shorter than its diff:
```python
import math

import jax
import jax.numpy as jnp
from jax import lax
from jax.sharding import PartitionSpec as P

HEAD_SIZE = 64


def matmul(left_side, right_side):
    return jnp.dot(left_side, right_side, preferred_element_type=jnp.float32)


def transposed_left(left_side, right_side):
    return lax.dot_general(
        left_side, right_side, (((0,), (0,)), ((), ())), preferred_element_type=jnp.float32
    )


def transposed_right(left_side, right_side):
    return lax.dot_general(
        left_side, right_side, (((1,), (1,)), ((), ())), preferred_element_type=jnp.float32
    )


def column_sum(values):
    return jnp.sum(values.astype(jnp.float32), axis=0)


def row_mean(values):
    return jnp.mean(values, axis=-1, keepdims=True)


def normalize(hidden):
    center = hidden - row_mean(hidden)
    inverse = lax.rsqrt(row_mean(center * center) + 1e-05)
    return center * inverse, inverse


def norm_back(grad, norm, inverse, gain):
    scaled = grad * gain
    return inverse * (scaled - row_mean(scaled) - norm * row_mean(scaled * norm))


def low(values):
    return values.astype(jnp.bfloat16)


def gather_small(biases, up_bias, gains):
    width, up_width = biases.shape[1], up_bias.shape[0]
    packed = jnp.concatenate([biases.reshape(-1), gains.reshape(-1), up_bias])
    everyone = lax.all_gather(packed, "fsdp", axis=0, tiled=False).astype(jnp.float32)
    rows = everyone[:, : 8 * width].reshape(-1, 8, width).transpose(1, 0, 2).reshape(8, -1)
    return rows[:6], everyone[:, 8 * width : 8 * width + up_width].reshape(-1), rows[6:]


def reduce_weight(grad):
    shard = lax.psum_scatter(low(grad), "fsdp", scatter_dimension=0, tiled=True)
    return lax.psum(shard, "rep").astype(jnp.float32)


def portable(
    tokens,
    lengths,
    cotangent,
    qkv_weight,
    out_weight,
    up_weight,
    down_weight,
    biases,
    up_bias,
    gains,
):
    slots = lengths.shape[0]
    rows, width = tokens.shape
    seq = rows // slots
    heads = width // HEAD_SIZE
    scale = 1.0 / math.sqrt(HEAD_SIZE)
    w_qkv = lax.all_gather(qkv_weight, "fsdp", axis=0, tiled=True)
    w_out = lax.all_gather(out_weight, "fsdp", axis=0, tiled=True)
    w_up = lax.all_gather(up_weight, "fsdp", axis=0, tiled=True)
    w_down = lax.all_gather(down_weight, "fsdp", axis=0, tiled=True)
    bias_rows, bias_up, gain_rows = gather_small(biases, up_bias, gains)

    def split(values):
        return values.reshape(slots, seq, heads, HEAD_SIZE)

    def join(values):
        return values.reshape(rows, width)

    sums = matmul(tokens, w_qkv)
    query = split(low(sums[:, :width] + bias_rows[0]))
    key = split(low(sums[:, width : 2 * width]))
    value = split(low(sums[:, 2 * width :] + bias_rows[1]))
    live = jnp.arange(seq)[None, :] < lengths[:, None]
    scores = scale * jnp.einsum(
        "bshd,bthd->bhst", query, key, preferred_element_type=jnp.float32
    )
    scores = jnp.where(live[:, None, None, :], scores, -1e30)
    exps = jnp.exp(scores - jnp.max(scores, axis=-1, keepdims=True))
    probs = exps / jnp.sum(exps, axis=-1, keepdims=True)
    probs_low = low(probs)
    mixed = low(
        join(jnp.einsum("bhst,bthd->bshd", probs_low, value, preferred_element_type=jnp.float32))
    )
    first, first_inverse = normalize(
        tokens.astype(jnp.float32) + matmul(mixed, w_out) + bias_rows[2]
    )
    first_norm = first * gain_rows[0] + bias_rows[3]
    first_low = low(first_norm)
    inner = matmul(first_low, w_up) + bias_up
    cumulative = 0.5 * (1.0 + lax.erf(inner * math.sqrt(0.5)))
    act_low = low(inner * cumulative)
    slope = low(cumulative + inner * jnp.exp(-0.5 * inner * inner) / math.sqrt(2.0 * math.pi))
    second, second_inverse = normalize(first_norm + matmul(act_low, w_down) + bias_rows[4])
    layer_out = low(second * gain_rows[1] + bias_rows[5])

    grad_out = cotangent * live.reshape(rows, 1).astype(jnp.float32)
    grad_h2 = norm_back(grad_out, second, second_inverse, gain_rows[1])
    grad_branch = low(grad_h2)
    down_grad = reduce_weight(transposed_left(act_low, grad_branch))
    grad_inner = low(transposed_right(grad_branch, w_down) * slope)
    up_grad = reduce_weight(transposed_left(first_low, grad_inner))
    grad_first = grad_h2 + transposed_right(grad_inner, w_up)
    grad_h1 = norm_back(grad_first, first, first_inverse, gain_rows[0])
    grad_attn = low(grad_h1)
    out_grad = reduce_weight(transposed_left(mixed, grad_attn))
    grad_mixed = split(low(transposed_right(grad_attn, w_out)))
    grad_probs = jnp.einsum(
        "bshd,bthd->bhst", grad_mixed, value, preferred_element_type=jnp.float32
    )
    shared = jnp.sum(probs * grad_probs, axis=-1, keepdims=True)
    grad_scores = low(probs * (grad_probs - shared))
    grad_query = scale * jnp.einsum(
        "bhst,bthd->bshd", grad_scores, key, preferred_element_type=jnp.float32
    )
    grad_key = scale * jnp.einsum(
        "bhst,bshd->bthd", grad_scores, query, preferred_element_type=jnp.float32
    )
    grad_value = jnp.einsum(
        "bhst,bshd->bthd", probs_low, grad_mixed, preferred_element_type=jnp.float32
    )
    grad_qkv = jnp.concatenate(
        [join(low(grad_query)), join(low(grad_key)), join(low(grad_value))], axis=1
    )
    qkv_grad = reduce_weight(transposed_left(tokens, grad_qkv))
    token_grad = grad_h1 + transposed_right(grad_qkv, w_qkv)
    small = jnp.stack(
        [
            column_sum(grad_qkv[:, :width]),
            column_sum(grad_qkv[:, 2 * width :]),
            column_sum(grad_attn),
            column_sum(grad_first),
            column_sum(grad_branch),
            column_sum(grad_out),
            column_sum(grad_first * first),
            column_sum(grad_out * second),
        ]
    )
    owner = lax.axis_index("fsdp")
    small, up_sum = lax.psum((small, column_sum(grad_inner)), ("fsdp", "rep"))
    own, own_up = biases.shape[1], up_bias.shape[0]
    small = lax.dynamic_slice(small, (0, owner * own), (8, own))
    up_bias_grad = lax.dynamic_slice(up_sum, (owner * own_up,), (own_up,))
    return (
        layer_out,
        token_grad,
        qkv_grad,
        out_grad,
        up_grad,
        down_grad,
        small[:6],
        up_bias_grad,
        small[6:],
    )


def solution(mesh):
    both = ("fsdp", "rep")
    in_specs = (
        P(both, None),
        P(both),
        P(both, None),
        P("fsdp", None),
        P("fsdp", None),
        P("fsdp", None),
        P("fsdp", None),
        P(None, "fsdp"),
        P("fsdp"),
        P(None, "fsdp"),
    )
    out_specs = (
        P(both, None),
        P(both, None),
        P("fsdp", None),
        P("fsdp", None),
        P("fsdp", None),
        P("fsdp", None),
        P(None, "fsdp"),
        P("fsdp"),
        P(None, "fsdp"),
    )
    return jax.shard_map(
        portable, mesh=mesh, in_specs=in_specs, out_specs=out_specs, check_vma=False
    )
```

time: 897 us -> 684 us (0.76)
  waiting for transfers between devices: 566 us -> 431 us
  matrix products: 174 us -> 112 us
  other arithmetic: 43.5 us -> 13.5 us
  local copies, waits for them, and re-layouts: 24.5 us -> 50.5 us
    reduce_scatter x5 -> x3, waiting for transfers between devices: 350 us -> 193 us  [reduce_weight(): shard = lax.psum_scatter(low(grad), 'fsdp', scatter_dimension=0, tiled=True)]
    psum x1, waiting for transfers between devices: 111 us -> 72 us  [reduce_weight(): return lax.psum(shard, 'rep').astype(jnp.float32)]
    unnamed x12 -> x10, waiting for transfers between devices: 2.7 us -> 38.8 us
    psum x1, blocking collectives: 11.8 us -> 44.2 us  [portable(): small, up_sum = lax.psum((small, column_sum(grad_inner)), ('fsdp', 'rep'))]
    all_gather x4, waiting for transfers between devices: 102 us -> 128 us  [the longest x1 45.7 us: portable(): w_down = lax.all_gather(down_weight, 'fsdp', axis=0, tiled=True)]
    dot_general x8 -> x4, matrix products: 52.1 us -> 28.4 us  [matmul(): return jnp.dot(left_side, right_side, preferred_element_type=jnp.float32)]
    unnamed x1 -> x0, blocking collectives: 23.5 us -> none
    reshape x0 -> x8, local copies, waits for them, and re-layouts: none -> 22.9 us  [split(): return values.reshape(slots, seq, heads, HEAD_SIZE)]
  transfers between devices with their start and end apart: 11 -> 9, of which waited for: 9 -> 8; matrix products, arithmetic and copies ran while one was open for 16% -> 13% of each run, Pallas kernels for 0% -> 0%
where the time goes in v1:
time: 684 us; the launch traced here: 677 us
  waiting for transfers between devices  431 us (63%)
  matrix products  112 us (16%)
  blocking collectives  54.8 us (8%)
  local copies, waits for them, and re-layouts  50.5 us (7%)
  between operations  14.8 us (2%)
  other arithmetic  13.5 us (2%)
    reduce_scatter x3, waiting for transfers between devices, reduce_weight(): shard = lax.psum_scatter(low(grad), 'fsdp', scatter_dimension=0, tiled=True)  193 us
    psum x1, waiting for transfers between devices, reduce_weight(): return lax.psum(shard, 'rep').astype(jnp.float32)  72 us
    all_gather x1, waiting for transfers between devices, portable(): w_down = lax.all_gather(down_weight, 'fsdp', axis=0, tiled=True)  45.7 us
    all_gather x1, waiting for transfers between devices, portable(): w_up = lax.all_gather(up_weight, 'fsdp', axis=0, tiled=True)  44.5 us
    psum x1, blocking collectives, portable(): small, up_sum = lax.psum((small, column_sum(grad_inner)), ('fsdp', 'rep'))  44.2 us
    unnamed x10, waiting for transfers between devices  38.8 us
    all_gather x1, waiting for transfers between devices, portable(): w_qkv = lax.all_gather(qkv_weight, 'fsdp', axis=0, tiled=True)  37.3 us
    dot_general x4, matrix products, transposed_right(): lax.dot_general(left_side, right_side, (((1,), (1,)), ((), ())), preferre...  31 us
  transfers between devices with their start and end apart: 9, of which 8 were waited for; matrix products, arithmetic and copies ran while one was open for 13% of the time, Pallas kernels for 0%

profile of v1, /device:TPU:0, one launch (start us, length us, event | category | flops | bytes accessed | tf_op | source)
XLA Modules:
  0.0 677.4 jit_solution(4580073348307100265)
XLA Ops:
  10.1 10.6 %all-gather.1 = bf16[8,1,1536]{2,1,0:T(2,128)(2,1)S(1)} all-gather(bf16[1,1,1536]{2,1,0:T(2,128)(2,1)S(1)} %reshape.165), channel_id=2, replica_groups=mesh['fsdp'=8,'rep'=4] {'fsdp'}, dimensions={0}, use_global_device_ids=true | all-gather | bytes 27648 | tf_op jit(solution)/shard_map/all_gather | solution.py:53
  20.9 37.3 %all-gather.7.cloned.1.call-done = bf16[1024,3072]{1,0:T(8,128)(2,1)} async-done(((bf16[128,3072]{1,0:T(8,128)(2,1)}), bf16[1024,3072]{1,0:T(8,128)(2,1)}) %all-gather.7.cloned.1.call-update) | async-done | bytes 6291472 | tf_op jit(solution)/shard_map/all_gather | solution.py:80
  58.2 5.5 fusion.45
  81.0 7.8 %fusion.42 = (f32[2,16,256]{2,1,0:T(8,128)S(1)}, f32[2,16,256,256]{2,3,1,0:T(8,128)}) fusion(pred[2,256]{1,0:T(4,128)(4,1)S(1)} %get-tuple-element.66, bf16[2,256,16,64]{1,3,2,0:T(8,128)(2,1)S(1)} %copy-done.1, bf16[2,256,16,64]{1,3,2,0:T(8,128)(2,1)} %copy.57), kind=kOutput, calls=%fused_computation.100 | convolution fusion | flops 276824320 | bytes 10519040 | tf_op jit(solution)/shard_map/sub | solution.py:101
  88.9 4.2 fusion.26
  99.9 44.5 %all-gather.11.cloned.1.call-done = bf16[1024,4096]{1,0:T(8,128)(2,1)} async-done(((bf16[128,4096]{1,0:T(8,128)(2,1)}), bf16[1024,4096]{1,0:T(8,128)(2,1)}) %all-gather.11.cloned.1.call-update) | async-done | bytes 8388624 | tf_op jit(solution)/shard_map/all_gather | solution.py:82
  144.3 10.5 %multiply_convert_fusion.2 = (bf16[512,4096]{1,0:T(8,128)(2,1)}, f32[512,4096]{1,0:T(8,128)}) fusion(f32[4096]{0:T(1024)S(1)} %bitcast.118, bf16[1024,4096]{1,0:T(8,128)(2,1)} %all-gather.11.cloned.1.call-done, f32[512,1024]{1,0:T(8,128)S(1)} %get-tuple-element.70, f32[1024]{0:T(1024)S(1)} %get-tuple-element.60, f32[1024]{0:T(1024)S(1)} %get-tuple-element.61, ...), kind=kOutput, calls=%fused_computation.11 | convolution fusion | flops 4310171648 | bytes 23097344 | tf_op jit(solution)/shard_map/dot_general | solution.py:12
  154.8 45.7 %all-gather.13.cloned.1.call-done = bf16[4096,1024]{1,0:T(8,128)(2,1)} async-done(((bf16[512,1024]{1,0:T(8,128)(2,1)}), bf16[4096,1024]{1,0:T(8,128)(2,1)}) %all-gather.13.cloned.1.call-update) | async-done | bytes 8388624 | tf_op jit(solution)/shard_map/all_gather | solution.py:83
  200.5 8.4 %fusion.44 = (f32[512]{0:T(512)S(1)}, f32[512,1024]{1,0:T(8,128)S(1)}) fusion(f32[1024]{0:T(1024)S(1)} %get-tuple-element.59, bf16[512,4096]{1,0:T(8,128)(2,1)} %get-tuple-element.71, bf16[4096,1024]{1,0:T(8,128)(2,1)} %all-gather.13.cloned.1.call-done, f32[1024]{0:T(1024)S(1)} %get-tuple-element.60, f32[1024]{0:T(1024)S(1)} %get-tuple-element.61, ...), kind=kOutput, calls=%fused_computation.102 | convolution fusion | flops 4298636800 | bytes 16795648 | tf_op jit(solution)/shard_map/dot_general | solution.py:12
  213.6 12.9 %convert_reduce_fusion = (f32[4096]{0:T(1024)S(1)}, bf16[512,4096]{1,0:T(8,128)(2,1)}) fusion(f32[512,4096]{1,0:T(8,128)} %get-tuple-element.72, f32[4096]{0:T(1024)S(1)} %bitcast.119, bf16[4096,1024]{1,0:T(8,128)(2,1)} %all-gather.13.cloned.1.call-done, f32[512,1024]{1,0:T(8,128)S(1)} %get-tuple-element.51), kind=kOutput, calls=%fused_computation.7 | convolution fusion | flops 4326944768 | bytes 23101440 | tf_op jit(solution)/shard_map/dot_general | solution.py:22
  226.5 7.2 %multiply_reduce_fusion.2 = (f32[1024]{0:T(1024)S(1)}, f32[512]{0:T(512)S(1)}, f32[512]{0:T(512)S(1)}, f32[1024]{0:T(1024)S(1)}, f32[512,1024]{1,0:T(8,128)S(1)}) fusion(f32[512,1024]{1,0:T(8,128)S(1)} %get-tuple-element.70, f32[512]{0:T(512)S(1)} %add_rsqrt_fusion.1, f32[512]{0:T(512)S(1)} %broadcast_multiply_fusion.5, f32[1024]{0:T(1024)S(1)} %get-tuple-element.61, ...), kind=kOutput, calls=%fused_computation.29 | convolution fusion | flops 4300207104 | bytes 18894848 | tf_op jit(solution)/shard_map/dot_general | solution.py:22
  245.9 5.3 convert_reduce_fusion.3
  251.3 5.0 multiply_reduce_fusion
  266.4 5.2 convert_bitcast_fusion
  271.6 8.7 %copy.78 = bf16[1024,3072]{1,0:T(8,128)(2,1)} copy(bf16[1024,3072]{0,1:T(8,128)(2,1)} %convert_bitcast_fusion) | data formatting | bytes 12582912
  285.7 9.6 %convolution_convert_fusion.1 = bf16[1024,4096]{1,0:T(8,128)(2,1)} fusion(bf16[512,4096]{1,0:T(8,128)(2,1)} %get-tuple-element.83, f32[512,1024]{1,0:T(8,128)S(1)} %get-tuple-element.70, f32[1024]{0:T(1024)S(1)} %get-tuple-element.60, f32[1024]{0:T(1024)S(1)} %get-tuple-element.61, f32[512]{0:T(512)S(1)} %add_rsqrt_fusion.1, ...), kind=kOutput, calls=%fused_computation.16 | convolution fusion | flops 4301783040 | bytes 14692352 | tf_op jit(solution)/shard_map/dot_general | solution.py:16
  297.0 9.0 %convolution_convert_fusion = bf16[4096,1024]{1,0:T(8,128)(2,1)} fusion(bf16[512,4096]{1,0:T(8,128)(2,1)} %get-tuple-element.71, f32[512,1024]{1,0:T(8,128)S(1)} %copy-done.8), kind=kOutput, calls=%fused_computation.15 | convolution fusion | flops 4299685888 | bytes 14680064 | tf_op jit(solution)/shard_map/dot_general | solution.py:16
  306.1 36.1 %reduce-scatter.13.cloned.1.call-done = bf16[128,3072]{1,0:T(8,128)(2,1)} async-done(((bf16[1024,3072]{1,0:T(8,128)(2,1)}), bf16[128,3072]{1,0:T(8,128)(2,1)}) %reduce-scatter.13.cloned.1.call-update) | async-done | bytes 786448
  344.5 43.0 %reduce-scatter.7.cloned.1.call-done = bf16[128,1024]{1,0:T(8,128)(2,1)} async-done(((bf16[1024,1024]{1,0:T(8,128)(2,1)}), bf16[128,1024]{1,0:T(8,128)(2,1)}) %reduce-scatter.7.cloned.1.call-update) | async-done | bytes 262160 | tf_op jit(solution)/shard_map/reduce_scatter | solution.py:59
  387.5 74.7 %reduce-scatter.9.cloned.1.call-done = bf16[128,4096]{1,0:T(8,128)(2,1)} async-done(((bf16[1024,4096]{1,0:T(8,128)(2,1)}), bf16[128,4096]{1,0:T(8,128)(2,1)}) %reduce-scatter.9.cloned.1.call-update) | async-done | bytes 1048592 | tf_op jit(solution)/shard_map/reduce_scatter | solution.py:59
  462.3 75.2 %reduce-scatter.11.cloned.1.call-done = bf16[512,1024]{1,0:T(8,128)(2,1)} async-done(((bf16[4096,1024]{1,0:T(8,128)(2,1)}), bf16[512,1024]{1,0:T(8,128)(2,1)}) %reduce-scatter.11.cloned.1.call-update) | async-done | bytes 1048592 | tf_op jit(solution)/shard_map/reduce_scatter | solution.py:59
  537.7 44.2 %all-reduce = (f32[8,1024]{1,0:T(8,128)S(1)}, f32[4096]{0:T(1024)S(1)}) all-reduce(f32[8,1024]{1,0:T(8,128)S(1)} %stack.35, f32[4096]{0:T(1024)S(1)} %get-tuple-element.82), channel_id=1, replica_groups=mesh['fsdp'=8,'rep'=4] {'fsdp','rep'}, use_global_device_ids=true, to_apply=%region_27.28 | all-reduce | flops 12288 | bytes 98304 | tf_op jit(solution)/shard_map/psum | solution.py:162
  583.2 8.5 %convolution_add_fusion = f32[512,1024]{1,0:T(8,128)} fusion(f32[512,1024]{1,0:T(8,128)S(1)} %copy-done.5, bf16[512,3072]{0,1:T(8,128)(2,1)} %copy-done.16, bf16[1024,3072]{1,0:T(8,128)(2,1)} %all-gather.7.cloned.1.call-done), kind=kOutput, calls=%fused_computation.57 | convolution fusion | flops 3221749760 | bytes 13631488 | tf_op jit(solution)/shard_map/dot_general | solution.py:22
  591.7 72.0 %all-reduce.4.cloned.1.call-done = (bf16[128,3072]{0,1:T(8,128)(2,1)}, bf16[128,1024]{1,0:T(8,128)(2,1)}, bf16[128,4096]{1,0:T(8,128)(2,1)}, bf16[512,1024]{1,0:T(8,128)(2,1)}) async-done(((bf16[128,3072]{0,1:T(8,128)(2,1)}, bf16[128,1024]{1,0:T(8,128)(2,1)}, bf16[128,4096]{1,0:T(8,128)(2,1)}, bf16[512,1024]{1,0:T(8,128)(2,1)}), (bf16[128,3072]{0,1:T(8,128)(2,1)}, bf16[128,1024]{1,0:T(8,128)(2,1)}, ...) | async-done | bytes 3145744 | tf_op jit(solution)/shard_map/psum | solution.py:60
  (134 shorter events, 71.2 us)
Async XLA Ops:
  7.2 2.9 copy-start.19
  7.2 13.6 %copy-start.21 = (s32[2]{0:T(128)S(1)}, s32[2]{0:T(128)}, u32[]{:S(2)}) copy-start(s32[2]{0:T(128)} %param.11) | copy-start | bytes 28
  7.2 51.0 %copy-start.13 = (bf16[512,1024]{1,0:T(8,128)(2,1)S(1)}, bf16[512,1024]{1,0:T(8,128)(2,1)}, u32[]{:S(2)}) copy-start(bf16[512,1024]{1,0:T(8,128)(2,1)} %param.10) | copy-start | bytes 3145732
  7.2 51.0 %all-gather.7.cloned.1.call-start = ((), (), s32[]{:S(2)}) async-start(), calls=%async_computation.4 | async-start | bytes 7077888 | tf_op jit(solution)/shard_map/all_gather | solution.py:80
  8.0 87.5 %all-gather.9.cloned.1.call-start = ((), (), s32[]{:S(2)}) async-start(), calls=%async_computation.5 | async-start | bytes 2359296 | tf_op jit(solution)/shard_map/all_gather | solution.py:81
  8.7 135.6 %all-gather.11.cloned.1.call-start = ((), (), s32[]{:S(2)}) async-start(), calls=%async_computation.6 | async-start | bytes 9437184 | tf_op jit(solution)/shard_map/all_gather | solution.py:82
  9.4 191.1 %all-gather.13.cloned.1.call-start = ((), (), s32[]{:S(2)}) async-start(), calls=%async_computation.7 | async-start | bytes 9437184 | tf_op jit(solution)/shard_map/all_gather | solution.py:83
  10.0 332.2 %reduce-scatter.13.cloned.1.call-start = ((), (), s32[]{:S(2)}) async-start(), calls=%async_computation.11 | async-start | bytes 7077888
  78.1 3.0 copy-start.1
  81.0 7.8 %copy-start.9 = (bf16[2,256,16,64]{1,3,2,0:T(8,128)(2,1)S(1)}, bf16[2,256,16,64]{1,3,2,0:T(8,128)(2,1)}, u32[]{:S(2)}) copy-start(bf16[2,256,16,64]{1,3,2,0:T(8,128)(2,1)} %copy.58) | copy-start | bytes 3145732
  211.6 14.9 %slice-start.2 = ((s8[8388608]{0:T(1024)(128)(4,1)}), s8[4194304]{0:T(1024)(128)(4,1)S(1)}, s32[]{:S(2)}) async-start(s8[8388608]{0:T(1024)(128)(4,1)} %bitcast.125), calls=%async_computation.15 | async-start | bytes 8388608
  213.6 12.9 %copy-start.7 = (f32[512,1024]{1,0:T(8,128)}, f32[512,1024]{1,0:T(8,128)S(1)}, u32[]{:S(2)}) copy-start(f32[512,1024]{1,0:T(8,128)S(1)} %get-tuple-element.51) | copy-start | bytes 6291460
  213.6 12.9 %slice-start.3 = ((s8[8388608]{0:T(1024)(128)(4,1)}), s8[4194304]{0:T(1024)(128)(4,1)S(1)}, s32[]{:S(2)}) async-start(s8[8388608]{0:T(1024)(128)(4,1)} %bitcast.125), calls=%async_computation.16 | async-start | bytes 8388608
  245.9 5.4 copy-start.10
  245.9 5.4 copy-start.12
  245.9 10.4 %slice-start = ((s8[8388608]{0:T(1024)(128)(4,1)}), s8[4194304]{0:T(1024)(128)(4,1)S(1)}, s32[]{:S(2)}) async-start(s8[8388608]{0:T(1024)(128)(4,1)} %bitcast.99), calls=%async_computation.13 | async-start | bytes 8388608
  251.3 5.1 slice-start.1
  280.3 107.2 %reduce-scatter.7.cloned.1.call-start = ((), (), s32[]{:S(2)}) async-start(), calls=%async_computation.8 | async-start | bytes 2359296 | tf_op jit(solution)/shard_map/reduce_scatter | solution.py:59
  285.7 176.6 %reduce-scatter.9.cloned.1.call-start = ((), (), s32[]{:S(2)}) async-start(), calls=%async_computation.9 | async-start | bytes 9437184 | tf_op jit(solution)/shard_map/reduce_scatter | solution.py:59
  295.4 242.1 %reduce-scatter.11.cloned.1.call-start = ((), (), s32[]{:S(2)}) async-start(), calls=%async_computation.10 | async-start | bytes 9437184 | tf_op jit(solution)/shard_map/reduce_scatter | solution.py:59
  306.0 277.2 %copy-start.5 = (f32[512,1024]{1,0:T(8,128)S(1)}, f32[512,1024]{1,0:T(8,128)}, u32[]{:S(2)}) copy-start(f32[512,1024]{1,0:T(8,128)} %copy-done.4) | copy-start | bytes 6291460
  306.0 357.7 %all-reduce.4.cloned.1.call-start = ((), (), s32[]{:S(2)}) async-start(), calls=%async_computation.12 | async-start | bytes 6291456 | tf_op jit(solution)/shard_map/psum | solution.py:60
  582.0 9.8 %copy-start.18 = (f32[8,128]{1,0:T(8,128)}, f32[8,128]{1,0:T(8,128)S(1)}, u32[]{:S(2)}) copy-start(f32[8,128]{1,0:T(8,128)S(1)} %constant_dynamic-slice_fusion) | copy-start | bytes 12292
  666.6 3.0 copy-start.17
  (12 other events, 23.3 us)
Sparse Core Ops, SparseCore 0:
  9.9 48.2 all-gather.6
  60.1 27.8 all-gather.8
  89.9 54.3 all-gather.10
  146.1 54.3 all-gather.12
  280.4 61.7 reduce-scatter.12
  346.3 41.2 reduce-scatter.6
  391.0 71.2 reduce-scatter.8
  466.1 71.2 reduce-scatter.10
  540.7 123.0 all-reduce.3

commit v2 on v1

--- a/solution.py
+++ b/solution.py
@@ -3,6 +3,8 @@
 import jax
 import jax.numpy as jnp
 from jax import lax
+from jax.experimental import pallas as pl
+from jax.experimental.pallas import tpu as pltpu
 from jax.sharding import PartitionSpec as P
 
 HEAD_SIZE = 64
@@ -176,7 +178,524 @@
     )
 
 
+MESH = pl.DeviceIdType.MESH
+F32 = jnp.float32
+BF16 = jnp.bfloat16
+MIB = 1 << 20
+
+
+def dot_nn(a, b):
+    return lax.dot_general(a, b, (((1,), (0,)), ((), ())), preferred_element_type=F32)
+
+
+def dot_nt(a, b):
+    return lax.dot_general(a, b, (((1,), (1,)), ((), ())), preferred_element_type=F32)
+
+
+def dot_tn(a, b):
+    return lax.dot_general(a, b, (((0,), (0,)), ((), ())), preferred_element_type=F32)
+
+
+class Place:
+    def __init__(self):
+        f, z = lax.axis_index("fsdp"), lax.axis_index("rep")
+        self.f, self.z = f, z
+        self.core = lax.rem(f, 2)
+        self.x = lax.rem(lax.div(f, 2), 2)
+        self.y = lax.div(f, 4)
+        self.chip = lax.div(f, 2)
+        self.fx = f + 2 - 4 * self.x
+        self.fy = f + 4 - 8 * self.y
+        self.fd = self.fx + 4 - 8 * self.y
+        self.fs = f + 1 - 2 * self.core
+        self.par = lax.rem(z, 2)
+        self.zn = z + 1 - 2 * self.par
+
+    def dev(self, f=None, z=None):
+        return {"fsdp": self.f if f is None else f, "rep": self.z if z is None else z}
+
+
+def remote(src, dst, send_sem, recv_sem, device):
+    return pltpu.make_async_remote_copy(
+        src_ref=src, dst_ref=dst, send_sem=send_sem, recv_sem=recv_sem,
+        device_id=device, device_id_type=MESH,
+    )
+
+
+UNITS = 4
+KINDS = 15
+
+
+class Gather:
+    def __init__(self, place, unit, shard, full, r, split, send, recv):
+        self.p, self.unit, self.shard, self.full = place, unit, shard, full
+        self.rows = shard.shape[0]
+        self.r, self.n = r, self.rows - r
+        self.h = split
+        self.lo = r * (1 - place.par)
+        self.z_out = self.n * (1 - place.par)
+        self.z_in = self.n * place.par
+        self.send, self.recv = send, recv
+
+    def at(self, f, lo, n):
+        return self.full.at[pl.ds(pl.multiple_of(f * self.rows + lo, 16), n)]
+
+    def copy(self, kind, f, lo, n, device, src=None):
+        place = self.at(f, lo, n)
+        return remote(
+            place if src is None else src, place,
+            self.send.at[self.unit, kind], self.recv.at[self.unit, kind], device,
+        )
+
+    def pieces(self):
+        p, lo, n, h, r = self.p, self.lo, self.n, self.h, self.r
+        to_x, to_y, to_s = p.dev(f=p.fx), p.dev(f=p.fy), p.dev(f=p.fs)
+        to_z = p.dev(z=p.zn)
+        sx, sy, sd = (g + 1 - 2 * p.core for g in (p.fx, p.fy, p.fd))
+        return {
+            0: (p.fx, p.f, lo, lo, n, to_x),
+            1: (p.fy, p.f, lo, lo, n, to_y),
+            2: (p.fd, p.fx, lo, lo, h, to_y),
+            3: (p.fd, p.fy, lo + h, lo + h, n - h, to_x),
+            4: (p.fx, p.fx, self.z_in, self.z_out, r, to_z),
+            5: (p.fy, p.fy, self.z_in, self.z_out, r, to_z),
+            6: (p.fd, p.fd, self.z_in, self.z_out, r, to_z),
+            7: (p.fs, p.f, 0, 0, self.rows, to_s),
+            8: (sx, p.fx, lo, lo, n, to_s),
+            9: (sx, p.fx, self.z_in, self.z_in, r, to_s),
+            10: (sy, p.fy, lo, lo, n, to_s),
+            11: (sy, p.fy, self.z_in, self.z_in, r, to_s),
+            12: (sd, p.fd, lo, lo, h, to_s),
+            13: (sd, p.fd, lo + h, lo + h, n - h, to_s),
+            14: (sd, p.fd, self.z_in, self.z_in, r, to_s),
+        }
+
+    def start(self, *kinds):
+        for kind in kinds:
+            _, owner, _, lo, n, device = self.pieces()[kind]
+            src = None
+            if kind in (0, 1, 7):
+                src = self.shard.at[pl.ds(pl.multiple_of(lo, 16), n)]
+            self.copy(kind, owner, lo, n, device, src).start()
+
+    def got(self, *kinds):
+        for kind in kinds:
+            owner, _, lo, _, n, device = self.pieces()[kind]
+            self.copy(kind, owner, lo, n, device).wait_recv()
+
+    def sent(self):
+        for kind in range(KINDS):
+            _, owner, _, lo, n, device = self.pieces()[kind]
+            self.copy(kind, owner, lo, n, device).wait_send()
+
+    def direct(self, local_sem):
+        self.start(0, 1, 7)
+        self.local(local_sem).start()
+
+    def local(self, local_sem):
+        return pltpu.make_async_copy(self.shard, self.at(self.p.f, 0, self.rows), local_sem)
+
+    def forward(self):
+        self.got(0)
+        self.start(2, 4, 8)
+        self.got(1)
+        self.start(3, 5, 10)
+
+    def finish(self):
+        self.got(2, 3)
+        self.start(6, 12, 13)
+        self.got(4)
+        self.start(9)
+        self.got(5)
+        self.start(11)
+        self.got(6)
+        self.start(14)
+        self.got(7, 8, 9, 10, 11, 12, 13, 14)
+
+
+def forward_kernel(
+    lengths, tokens, cot, small, sh_q, sh_o, sh_u, sh_d,
+    layer_out, wq_out, wo_out, wu_out, wd_out, qkv_out, slope_out, act_pair, first_pair, mixed_pair,
+    tok_pair, branch_pair, norm_out, inv_out, grad_out_ref, params_out, sums_out, act_out, mixed_out,
+    x, wq, wo, wu, wd, qkv, mixed, norm, first_low, act, slope, acc, cot_v, gh2, out_v, gb, smalls, params,
+    inv_v, sums, up_rows,
+    ag_send, ag_recv, ag_local, sm_send, sm_recv, sm_local, io, pair_send, pair_recv, pair_local,
+):
+    p = Place()
+    rows, width = x.shape
+    slots = lengths.shape[0]
+    seq = rows // slots
+    others = [lax.rem(p.f + k, 8) for k in range(1, 8)]
+    barrier = pltpu.get_barrier_semaphore()
+    for g in others:
+        pl.semaphore_signal(barrier, inc=1, device_id=p.dev(f=g), device_id_type=MESH)
+    pl.semaphore_signal(barrier, inc=1, device_id=p.dev(z=p.zn), device_id_type=MESH)
+    loads = [
+        pltpu.make_async_copy(tokens, x, io.at[0]),
+        pltpu.make_async_copy(cot, cot_v, io.at[1]),
+        pltpu.make_async_copy(small, smalls.at[p.f], sm_local),
+    ]
+    for c in loads:
+        c.start()
+    pl.semaphore_wait(barrier, 8)
+
+    def small_copy(k, owner, device):
+        return remote(small, smalls.at[owner], sm_send.at[k], sm_recv.at[k], device)
+
+    for k, g in enumerate(others):
+        small_copy(k, p.f, p.dev(f=g)).start()
+
+    shards = (sh_q, sh_o, sh_u, sh_d)
+    fulls = (wq, wo, wu, wd)
+    cuts = ((32, 48), (32, 48), (32, 48), (160, 176))
+    g_q, g_o, g_u, g_d = (
+        Gather(p, u, shards[u], fulls[u], *cuts[u], ag_send, ag_recv) for u in range(UNITS)
+    )
+    g_q.direct(ag_local.at[0])
+    g_o.direct(ag_local.at[1])
+
+    mine = pl.ds(pl.multiple_of(p.core * rows, rows), rows)
+
+    def pair(index, chip, src, dst, cols):
+        own = pl.ds(pl.multiple_of((2 * chip + p.core) * cols, cols), cols)
+        other = pl.ds(pl.multiple_of((2 * chip + 1 - p.core) * cols, cols), cols)
+        here = dst.at[mine, pl.ds(chip * cols, cols)]
+        return (
+            pltpu.make_async_copy(src.at[:, own], here, pair_local.at[index, chip]),
+            remote(src.at[:, other], here, pair_send.at[index, chip], pair_recv.at[index, chip], p.dev(f=p.fs)),
+        )
+
+    pairs = []
+
+    def start_pair(index, src, dst, cols, chips=range(4)):
+        for chip in chips:
+            for c in pair(index, chip, src, dst, cols):
+                c.start()
+            pairs.append((index, chip, src, dst, cols))
+
+    loads[0].wait()
+    start_pair(0, x, tok_pair, 128)
+    loads[2].wait()
+    for k, g in enumerate(others):
+        back = lax.rem(p.f + 7 - k, 8)
+        small_copy(k, back, p.dev(f=back)).wait_recv()
+    for g in range(8):
+        part = smalls[g].astype(F32)
+        params[:, g * 128 : (g + 1) * 128] = part
+        for j in range(4):
+            up_rows[g : g + 1, j * 128 : (j + 1) * 128] = part[8 + j : 9 + j]
+    g_q.forward()
+    g_o.forward()
+    g_u.direct(ag_local.at[2])
+    g_q.finish()
+    g_q.local(ag_local.at[0]).wait()
+    stores = [pltpu.make_async_copy(wq, wq_out, io.at[2])]
+    stores[-1].start()
+    for j in range(3):
+        part = dot_nn(x[...], wq[:, j * width : (j + 1) * width])
+        if j == 0:
+            part = part + params[0:1]
+        if j == 2:
+            part = part + params[1:2]
+        qkv[:, j * width : (j + 1) * width] = part.astype(BF16)
+    stores.append(pltpu.make_async_copy(qkv, qkv_out, io.at[3]))
+    stores[-1].start()
+
+    left = lax.broadcasted_iota(jnp.int32, (seq, 128), 1) < HEAD_SIZE
+    key_row = lax.broadcasted_iota(jnp.int32, (seq, seq), 0)
+
+    def attend(step, carry):
+        slot, pair_of = lax.div(step, 8), lax.rem(step, 8)
+        at_rows = pl.ds(pl.multiple_of(slot * seq, seq), seq)
+        col = pl.multiple_of(pair_of * 128, 128)
+        q = qkv[at_rows, pl.ds(col, 128)]
+        k = qkv[at_rows, pl.ds(pl.multiple_of(width + col, 128), 128)]
+        v = qkv[at_rows, pl.ds(pl.multiple_of(2 * width + col, 128), 128)]
+        dead = key_row >= lengths[slot]
+        outs = []
+        for head in range(2):
+            k_head = jnp.where(left if head == 0 else ~left, k, jnp.zeros_like(k))
+            scores = dot_nt(k_head, q) * (1.0 / math.sqrt(HEAD_SIZE))
+            scores = jnp.where(dead, -1e30, scores)
+            exps = jnp.exp(scores - jnp.max(scores, axis=0, keepdims=True))
+            probs = exps * (1.0 / jnp.sum(exps, axis=0, keepdims=True))
+            outs.append(dot_tn(probs.astype(BF16), v))
+        mixed[at_rows, pl.ds(col, 128)] = jnp.where(left, outs[0], outs[1]).astype(BF16)
+        return carry
+
+    lax.fori_loop(0, 8 * slots, attend, 0)
+    start_pair(1, mixed, mixed_pair, 128)
+    g_o.finish()
+    g_o.local(ag_local.at[1]).wait()
+    g_u.forward()
+    g_d.direct(ag_local.at[3])
+    stores.append(pltpu.make_async_copy(wo, wo_out, io.at[4]))
+    stores[-1].start()
+    hidden = x[...].astype(F32) + dot_nn(mixed[...], wo[...]) + params[2:3]
+    center = hidden - row_mean(hidden)
+    inverse = lax.rsqrt(row_mean(center * center) + 1e-05)
+    norm[...] = center * inverse
+    inv_v[...] = jnp.broadcast_to(inverse, inv_v.shape)
+    acc[...] = norm[...] * params[6:7] + params[3:4]
+    first_low[...] = acc[...].astype(BF16)
+    start_pair(2, first_low, first_pair, 128)
+    stores.append(pltpu.make_async_copy(norm, norm_out, io.at[5]))
+    stores.append(pltpu.make_async_copy(inv_v, inv_out, io.at[6]))
+    stores[-1].start()
+    stores[-2].start()
+    g_u.finish()
+    g_u.local(ag_local.at[2]).wait()
+    stores.append(pltpu.make_async_copy(wu, wu_out, io.at[7]))
+    stores[-1].start()
+
+    def up_step(j, carry):
+        cols = pl.ds(pl.multiple_of(j * 512, 512), 512)
+        inner = dot_nn(first_low[...], wu[:, cols]) + up_rows[pl.ds(j, 1), :]
+        phi = 0.5 * (1.0 + lax.erf(inner * math.sqrt(0.5)))
+        act[:, cols] = (inner * phi).astype(BF16)
+        density = jnp.exp(-0.5 * inner * inner) * (1.0 / math.sqrt(2.0 * math.pi))
+        slope[:, cols] = (phi + inner * density).astype(BF16)
+        return carry
+
+    lax.fori_loop(0, 4, up_step, 0)
+    g_d.forward()
+    start_pair(3, act, act_pair, 512, range(2))
+    lax.fori_loop(4, 8, up_step, 0)
+    start_pair(3, act, act_pair, 512, range(2, 4))
+    stores.append(pltpu.make_async_copy(slope, slope_out, io.at[8]))
+    stores[-1].start()
+    stores.append(pltpu.make_async_copy(act, act_out, io.at[14]))
+    stores[-1].start()
+    stores.append(pltpu.make_async_copy(mixed, mixed_out, io.at[15]))
+    stores[-1].start()
+    g_d.finish()
+    g_d.local(ag_local.at[3]).wait()
+    stores.append(pltpu.make_async_copy(wd, wd_out, io.at[9]))
+    stores[-1].start()
+    acc[...] += params[4:5]
+    for j in range(4):
+        acc[...] += dot_nn(act[:, j * 1024 : (j + 1) * 1024], wd[j * 1024 : (j + 1) * 1024, :])
+    loads[1].wait()
+    hidden = acc[...]
+    center = hidden - row_mean(hidden)
+    inverse = lax.rsqrt(row_mean(center * center) + 1e-05)
+    second = center * inverse
+    out_v[...] = (second * params[7:8] + params[5:6]).astype(BF16)
+    stores.append(pltpu.make_async_copy(out_v, layer_out, io.at[10]))
+    stores[-1].start()
+    row_at = lax.broadcasted_iota(jnp.int32, (seq, 1), 0)
+    live = jnp.concatenate([(row_at < lengths[s]).astype(F32) for s in range(slots)], axis=0)
+    e = cot_v[...] * live
+    sums[...] = jnp.zeros_like(sums)
+    sums[0:1] = jnp.sum(e * second, axis=0, keepdims=True)
+    sums[1:2] = jnp.sum(e, axis=0, keepdims=True)
+    scaled = e * params[7:8]
+    gh2[...] = inverse * (scaled - row_mean(scaled) - second * row_mean(scaled * second))
+    gb[...] = gh2[...].astype(BF16)
+    c_local = pltpu.make_async_copy(gb, branch_pair.at[mine], pair_local.at[4, 0])
+    c_remote = remote(gb, branch_pair.at[mine], pair_send.at[4, 0], pair_recv.at[4, 0], p.dev(f=p.fs))
+    c_local.start()
+    c_remote.start()
+    sums[2:3] = jnp.sum(gb[...].astype(F32), axis=0, keepdims=True)
+    stores.append(pltpu.make_async_copy(gh2, grad_out_ref, io.at[11]))
+    stores.append(pltpu.make_async_copy(params, params_out, io.at[12]))
+    stores.append(pltpu.make_async_copy(sums, sums_out, io.at[13]))
+    for c in stores[-3:]:
+        c.start()
+    for c in stores:
+        c.wait()
+    c_local.wait()
+    c_remote.wait()
+    for args in pairs:
+        a, b = pair(*args)
+        a.wait()
+        b.wait()
+    for k, g in enumerate(others):
+        small_copy(k, p.f, p.dev(f=g)).wait_send()
+    for g in (g_q, g_o, g_u, g_d):
+        g.sent()
+
+
+def forward_call(tokens, lengths, cotangent, qkv_w, out_w, up_w, down_w, small):
+    rows, width = tokens.shape
+    ff = up_w.shape[1]
+    anyspace = pl.BlockSpec(memory_space=pl.ANY)
+    shape = jax.ShapeDtypeStruct
+    outs = [
+        shape((rows, width), BF16),
+        shape((width, 3 * width), BF16),
+        shape((width, width), BF16),
+        shape((width, ff), BF16),
+        shape((ff, width), BF16),
+        shape((rows, 3 * width), BF16),
+        shape((rows, ff), BF16),
+        shape((2 * rows, ff // 2), BF16),
+        shape((2 * rows, width // 2), BF16),
+        shape((2 * rows, width // 2), BF16),
+        shape((2 * rows, width // 2), BF16),
+        shape((2 * rows, width), BF16),
+        shape((rows, width), F32),
+        shape((rows, 128), F32),
+        shape((rows, width), F32),
+        shape((16, width), F32),
+        shape((8, width), F32),
+        shape((rows, ff), BF16),
+        shape((rows, width), BF16),
+    ]
+    dma = pltpu.SemaphoreType.DMA
+    scratch = [
+        pltpu.VMEM((rows, width), BF16),
+        pltpu.VMEM((width, 3 * width), BF16),
+        pltpu.VMEM((width, width), BF16),
+        pltpu.VMEM((width, ff), BF16),
+        pltpu.VMEM((ff, width), BF16),
+        pltpu.VMEM((rows, 3 * width), BF16),
+        pltpu.VMEM((rows, width), BF16),
+        pltpu.VMEM((rows, width), F32),
+        pltpu.VMEM((rows, width), BF16),
+        pltpu.VMEM((rows, ff), BF16),
+        pltpu.VMEM((rows, ff), BF16),
+        pltpu.VMEM((rows, width), F32),
+        pltpu.VMEM((rows, width), F32),
+        pltpu.VMEM((rows, width), F32),
+        pltpu.VMEM((rows, width), BF16),
+        pltpu.VMEM((rows, width), BF16),
+        pltpu.VMEM((8, 16, 128), BF16),
+        pltpu.VMEM((16, width), F32),
+        pltpu.VMEM((rows, 128), F32),
+        pltpu.VMEM((8, width), F32),
+        pltpu.VMEM((8, ff // 8), F32),
+        dma((UNITS, KINDS)),
+        dma((UNITS, KINDS)),
+        dma((UNITS,)),
+        dma((7,)),
+        dma((7,)),
+        dma,
+        dma((16,)),
+        dma((5, 4)),
+        dma((5, 4)),
+        dma((5, 4)),
+    ]
+    return pl.pallas_call(
+        forward_kernel,
+        out_shape=outs,
+        in_specs=[pl.BlockSpec(memory_space=pltpu.SMEM)] + [anyspace] * 7,
+        out_specs=[anyspace] * len(outs),
+        scratch_shapes=scratch,
+        name="forward",
+        cost_estimate=pl.CostEstimate(flops=2 * 512 * 12582912, bytes_accessed=60 * MIB, transcendentals=4 * MIB),
+        compiler_params=pltpu.CompilerParams(
+            collective_id=0, has_side_effects=True, vmem_limit_bytes=60 * MIB
+        ),
+    )(lengths, tokens, cotangent, small, qkv_w, out_w, up_w, down_w)
+
+
+def pack_small(biases, up_bias, gains):
+    return jnp.concatenate([biases, gains, up_bias.reshape(4, 128), jnp.zeros((4, 128), BF16)], axis=0)
+
+
+def plane(
+    tokens,
+    lengths,
+    cotangent,
+    qkv_weight,
+    out_weight,
+    up_weight,
+    down_weight,
+    biases,
+    up_bias,
+    gains,
+):
+    slots = lengths.shape[0]
+    rows, width = tokens.shape
+    seq = rows // slots
+    heads = width // HEAD_SIZE
+    scale = 1.0 / math.sqrt(HEAD_SIZE)
+    got = forward_call(
+        tokens, lengths, cotangent, qkv_weight, out_weight, up_weight, down_weight,
+        pack_small(biases, up_bias, gains),
+    )
+    layer_out, w_qkv, w_out, w_up, w_down, qkv, slope = got[:7]
+    grad_branch_pair, first, first_inverse, grad_h2, params, sums, act_low, mixed = got[11:]
+    first_inverse = first_inverse[:, :1]
+    gain_one = params[6]
+    first_low = low(first * gain_one + params[3])
+    grad_branch = low(grad_h2)
+
+    def split(values):
+        return values.reshape(slots, seq, heads, HEAD_SIZE)
+
+    def join(values):
+        return values.reshape(rows, width)
+
+    query, key, value = (split(qkv[:, j * width : (j + 1) * width]) for j in range(3))
+    live = jnp.arange(seq)[None, :] < lengths[:, None]
+    scores = scale * jnp.einsum(
+        "bshd,bthd->bhst", query, key, preferred_element_type=jnp.float32
+    )
+    scores = jnp.where(live[:, None, None, :], scores, -1e30)
+    exps = jnp.exp(scores - jnp.max(scores, axis=-1, keepdims=True))
+    probs = exps / jnp.sum(exps, axis=-1, keepdims=True)
+    probs_low = low(probs)
+    down_grad = reduce_weight(transposed_left(act_low, grad_branch))
+    grad_inner = low(transposed_right(grad_branch, w_down) * slope)
+    up_grad = reduce_weight(transposed_left(first_low, grad_inner))
+    grad_first = grad_h2 + transposed_right(grad_inner, w_up)
+    grad_h1 = norm_back(grad_first, first, first_inverse, gain_one)
+    grad_attn = low(grad_h1)
+    out_grad = reduce_weight(transposed_left(mixed, grad_attn))
+    grad_mixed = split(low(transposed_right(grad_attn, w_out)))
+    grad_probs = jnp.einsum(
+        "bshd,bthd->bhst", grad_mixed, value, preferred_element_type=jnp.float32
+    )
+    shared = jnp.sum(probs * grad_probs, axis=-1, keepdims=True)
+    grad_scores = low(probs * (grad_probs - shared))
+    grad_query = scale * jnp.einsum(
+        "bhst,bthd->bshd", grad_scores, key, preferred_element_type=jnp.float32
+    )
+    grad_key = scale * jnp.einsum(
+        "bhst,bshd->bthd", grad_scores, query, preferred_element_type=jnp.float32
+    )
+    grad_value = jnp.einsum(
+        "bhst,bshd->bthd", probs_low, grad_mixed, preferred_element_type=jnp.float32
+    )
+    grad_qkv = jnp.concatenate(
+        [join(low(grad_query)), join(low(grad_key)), join(low(grad_value))], axis=1
+    )
+    qkv_grad = reduce_weight(transposed_left(tokens, grad_qkv))
+    token_grad = grad_h1 + transposed_right(grad_qkv, w_qkv)
+    small = jnp.stack(
+        [
+            column_sum(grad_qkv[:, :width]),
+            column_sum(grad_qkv[:, 2 * width :]),
+            column_sum(grad_attn),
+            column_sum(grad_first),
+            sums[2],
+            sums[1],
+            column_sum(grad_first * first),
+            sums[0],
+        ]
+    )
+    owner = lax.axis_index("fsdp")
+    small, up_sum = lax.psum((small, column_sum(grad_inner)), ("fsdp", "rep"))
+    own, own_up = biases.shape[1], up_bias.shape[0]
+    small = lax.dynamic_slice(small, (0, owner * own), (8, own))
+    up_bias_grad = lax.dynamic_slice(up_sum, (owner * own_up,), (own_up,))
+    return (
+        layer_out,
+        token_grad,
+        qkv_grad,
+        out_grad,
+        up_grad,
+        down_grad,
+        small[:6],
+        up_bias_grad,
+        small[6:],
+    )
+
+
 def solution(mesh):
+    step = plane if dict(mesh.shape) == {"fsdp": 8, "rep": 4} else portable
     both = ("fsdp", "rep")
     in_specs = (
         P(both, None),
@@ -202,5 +721,5 @@
         P(None, "fsdp"),
     )
     return jax.shard_map(
-        portable, mesh=mesh, in_specs=in_specs, out_specs=out_specs, check_vma=False
-    )
+        step, mesh=mesh, in_specs=in_specs, out_specs=out_specs, check_vma=False
+    )

time: 684 us -> 615 us (0.90)
  waiting for transfers between devices: 431 us -> 297 us
  Pallas kernels: 0 us -> 121 us
  matrix products: 112 us -> 73.4 us
  blocking collectives: 54.8 us -> 44.2 us
    all_gather x4 -> x0, waiting for transfers between devices: 128 us -> none  [the longest x1 45.7 us: portable(): w_down = lax.all_gather(down_weight, 'fsdp', axis=0, tiled=True)]
    pallas_call x0 -> x1, Pallas kernels: none -> 121 us  [forward_call(): pl.pallas_call(forward_kernel, out_shape=outs, in_specs=[pl.BlockSpec(mem...]
    dot_general x9 -> x4, matrix products: 45.4 us -> 9.11 us  [the longest x1 5 us: plane(): jnp.einsum('bhst,bshd->bthd', probs_low, grad_mixed, preferred_element_ty...]
    all_gather x1 -> x0, blocking collectives: 10.6 us -> none  [gather_small(): lax.all_gather(packed, 'fsdp', axis=0, tiled=False).astype(jnp.float32)]
    reshape x8 -> x7, local copies, waits for them, and re-layouts: 22.9 us -> 16.4 us  [split(): return values.reshape(slots, seq, heads, HEAD_SIZE)]
    unnamed x10 -> x6, waiting for transfers between devices: 38.8 us -> 33.3 us
    unnamed x68 -> x45, local copies, waits for them, and re-layouts: 21.5 us -> 20.3 us
  transfers between devices with their start and end apart: 9 -> 5, of which waited for: 8 -> 5; matrix products, arithmetic and copies ran while one was open for 13% -> 6% of each run, Pallas kernels for 0% -> 0%
where the time goes in v2:
time: 615 us; the launch traced here: 609 us
  waiting for transfers between devices  297 us (48%)
  Pallas kernels  121 us (20%)
  matrix products  73.4 us (12%)
  local copies, waits for them, and re-layouts  47.8 us (8%)
  blocking collectives  44.2 us (7%)
  between operations  14.6 us (2%)
  other arithmetic  9.9 us (2%)
    reduce_scatter x3, waiting for transfers between devices, reduce_weight(): shard = lax.psum_scatter(low(grad), 'fsdp', scatter_dimension=0, tiled=True)  193 us
    pallas_call x1, Pallas kernels, forward_call(): pl.pallas_call(forward_kernel, out_shape=outs, in_specs=[pl.BlockSpec(mem...  121 us
    psum x1, waiting for transfers between devices, reduce_weight(): return lax.psum(shard, 'rep').astype(jnp.float32)  71.1 us
    psum x1, blocking collectives, plane(): small, up_sum = lax.psum((small, column_sum(grad_inner)), ('fsdp', 'rep'))  44.2 us
    unnamed x6, waiting for transfers between devices  33.3 us
    dot_general x4, matrix products, transposed_left(): lax.dot_general(left_side, right_side, (((0,), (0,)), ((), ())), preferre...  30.1 us
    dot_general x4, matrix products, transposed_right(): lax.dot_general(left_side, right_side, (((1,), (1,)), ((), ())), preferre...  28.9 us
    unnamed x45, local copies, waits for them, and re-layouts  20.3 us
  transfers between devices with their start and end apart: 5, of which 5 were waited for; matrix products, arithmetic and copies ran while one was open for 6% of the time, Pallas kernels for 0%

profile of v2, /device:TPU:0, one launch (start us, length us, event | category | flops | bytes accessed | tf_op | source)
XLA Modules:
  0.0 608.7 jit_solution(2823733548032383555)
XLA Ops:
  9.4 121.1 %forward.1 = (bf16[512,1024]{1,0:T(8,128)(2,1)}, bf16[1024,3072]{1,0:T(8,128)(2,1)}, bf16[1024,1024]{1,0:T(8,128)(2,1)}, bf16[1024,4096]{1,0:T(8,128)(2,1)}, bf1...) custom-call(s32[2]{0:T(128)} %lengths.1, ...), custom_call_target="tpu_custom_call" | custom-call | flops 12884901888 | bytes 62914560 | tf_op jit(solution)/shard_map/forward/pallas_call | solution.py:579
  132.5 9.9 %convert_reduce_fusion = (f32[4096]{0:T(1024)S(1)}, bf16[512,4096]{1,0:T(8,128)(2,1)S(1)}) fusion(bf16[512,4096]{1,0:T(8,128)(2,1)} %get-tuple-element.27, bf16[4096,1024]{1,0:T(8,128)(2,1)} %get-tuple-element.26, f32[512,1024]{1,0:T(8,128)} %get-tuple-element.25), kind=kOutput, calls=%fused_computation.1 | convolution fusion | flops 4305973248 | bytes 18890752 | tf_op jit(solution)/shard_map/dot_general | solution.py:24
  142.4 9.2 %multiply_reduce_fusion.1 = (f32[1024]{0:T(1024)S(1)}, f32[512]{0:T(512)S(1)}, f32[512]{0:T(512)S(1)}, f32[1024]{0:T(1024)S(1)}, f32[512,1024]{1,0:T(8,128)S(1)}) fusion(f32[512,1024]{1,0:T(8,128)S(1)} %copy-done.5, f32[1024]{0:T(1024)S(1)} %bitcast.59, f32[512,1024]{1,0:T(8,128)S(1)} %copy-done.17, bf16[512,4096]{1,0:T(8,128)(2,1)S(1)} %get-tuple-element.94, ...), kind=kOutput, calls=%fused_computation.19 | convolution fusion | flops 4299158528 | bytes 18890752 | tf_op jit(solution)/shard_map/dot_general | solution.py:24
  156.2 2.5 copy.54
  158.7 3.5 fusion.27
  165.2 3.0 reshape.85
  168.1 2.5 copy.56
  170.6 4.1 reshape.82
  174.7 5.3 fusion.30
  180.0 5.0 convert_reduce_fusion.2
  198.4 5.3 convert_bitcast_fusion
  203.7 8.6 %copy.71 = bf16[1024,3072]{1,0:T(8,128)(2,1)} copy(bf16[1024,3072]{0,1:T(8,128)(2,1)} %convert_bitcast_fusion) | data formatting | bytes 12582912
  214.2 2.6 convolution_convert_fusion.2
  217.1 11.5 %convolution_convert_fusion.1 = bf16[1024,4096]{1,0:T(8,128)(2,1)} fusion(bf16[512,4096]{1,0:T(8,128)(2,1)} %copy-done.16, f32[512,1024]{1,0:T(8,128)} %get-tuple-element.30, f32[1024]{0:T(1024)S(1)} %bitcast.65, f32[1024]{0:T(1024)S(1)} %bitcast.61), kind=kOutput, calls=%fused_computation.8 | convolution fusion | flops 4300734464 | bytes 14688256 | tf_op jit(solution)/shard_map/dot_general | solution.py:18
  228.7 10.7 %convolution_convert_fusion = bf16[4096,1024]{1,0:T(8,128)(2,1)} fusion(bf16[512,4096]{1,0:T(8,128)(2,1)} %get-tuple-element.35, f32[512,1024]{1,0:T(8,128)} %get-tuple-element.25), kind=kOutput, calls=%fused_computation.7 | convolution fusion | flops 4299685888 | bytes 14680064 | tf_op jit(solution)/shard_map/dot_general | solution.py:18
  239.4 33.2 %reduce-scatter.13.cloned.1.call-done = bf16[128,3072]{1,0:T(8,128)(2,1)} async-done(((bf16[1024,3072]{1,0:T(8,128)(2,1)}), bf16[128,3072]{1,0:T(8,128)(2,1)}) %reduce-scatter.13.cloned.1.call-update) | async-done | bytes 786448
  272.6 2.3 copy.72
  274.9 43.2 %reduce-scatter.7.cloned.1.call-done = bf16[128,1024]{1,0:T(8,128)(2,1)} async-done(((bf16[1024,1024]{1,0:T(8,128)(2,1)}), bf16[128,1024]{1,0:T(8,128)(2,1)}) %reduce-scatter.7.cloned.1.call-update) | async-done | bytes 262160 | tf_op jit(solution)/shard_map/reduce_scatter | solution.py:61
  318.0 74.8 %reduce-scatter.9.cloned.1.call-done = bf16[128,4096]{1,0:T(8,128)(2,1)} async-done(((bf16[1024,4096]{1,0:T(8,128)(2,1)}), bf16[128,4096]{1,0:T(8,128)(2,1)}) %reduce-scatter.9.cloned.1.call-update) | async-done | bytes 1048592 | tf_op jit(solution)/shard_map/reduce_scatter | solution.py:61
  392.8 75.0 %reduce-scatter.11.cloned.1.call-done = bf16[512,1024]{1,0:T(8,128)(2,1)} async-done(((bf16[4096,1024]{1,0:T(8,128)(2,1)}), bf16[512,1024]{1,0:T(8,128)(2,1)}) %reduce-scatter.11.cloned.1.call-update) | async-done | bytes 1048592 | tf_op jit(solution)/shard_map/reduce_scatter | solution.py:61
  468.9 44.2 %all-reduce = (f32[8,1024]{1,0:T(8,128)S(1)}, f32[4096]{0:T(1024)S(1)}) all-reduce(f32[8,1024]{1,0:T(8,128)S(1)} %stack.23, f32[4096]{0:T(1024)S(1)} %get-tuple-element.93), channel_id=1, replica_groups=mesh['fsdp'=8,'rep'=4] {'fsdp','rep'}, use_global_device_ids=true, to_apply=%region_18.19 | all-reduce | flops 12288 | bytes 98304 | tf_op jit(solution)/shard_map/psum | solution.py:680
  514.3 8.5 %convolution_add_fusion = f32[512,1024]{1,0:T(8,128)} fusion(f32[512,1024]{1,0:T(8,128)S(1)} %copy-done.4, bf16[512,3072]{0,1:T(8,128)(2,1)} %copy-done.10, bf16[1024,3072]{1,0:T(8,128)(2,1)} %get-tuple-element.33), kind=kOutput, calls=%fused_computation.30 | convolution fusion | flops 3221749760 | bytes 13631488 | tf_op jit(solution)/shard_map/dot_general | solution.py:24
  522.9 71.1 %all-reduce.4.cloned.1.call-done = (bf16[128,3072]{0,1:T(8,128)(2,1)}, bf16[128,1024]{1,0:T(8,128)(2,1)}, bf16[128,4096]{1,0:T(8,128)(2,1)}, bf16[512,1024]{1,0:T(8,128)(2,1)}) async-done(((bf16[128,3072]{0,1:T(8,128)(2,1)}, bf16[128,1024]{1,0:T(8,128)(2,1)}, bf16[128,4096]{1,0:T(8,128)(2,1)}, bf16[512,1024]{1,0:T(8,128)(2,1)}), (bf16[128,3072]{0,1:T(8,128)(2,1)}, bf16[128,1024]{1,0:T(8,128)(2,1)}, ...) | async-done | bytes 3145744 | tf_op jit(solution)/shard_map/psum | solution.py:62
  593.9 2.9 convert_element_type.103
  (82 shorter events, 34.3 us)
Async XLA Ops:
  7.2 265.4 %reduce-scatter.13.cloned.1.call-start = ((), (), s32[]{:S(2)}) async-start(), calls=%async_computation.7 | async-start | bytes 7077888
  132.4 9.9 %copy-start.5 = (f32[512,1024]{1,0:T(8,128)S(1)}, f32[512,1024]{1,0:T(8,128)}, u32[]{:S(2)}) copy-start(f32[512,1024]{1,0:T(8,128)} %get-tuple-element.30) | copy-start | bytes 6291460
  132.4 9.9 %copy-start.17 = (f32[512,1024]{1,0:T(8,128)S(1)}, f32[512,1024]{1,0:T(8,128)}, u32[]{:S(2)}) copy-start(f32[512,1024]{1,0:T(8,128)} %get-tuple-element.25) | copy-start | bytes 6291460
  142.3 9.3 %copy-start.16 = (bf16[512,4096]{1,0:T(8,128)(2,1)}, bf16[512,4096]{1,0:T(8,128)(2,1)S(1)}, u32[]{:S(2)}) copy-start(bf16[512,4096]{1,0:T(8,128)(2,1)S(1)} %get-tuple-element.94) | copy-start | bytes 12582916
  151.6 1.9 copy-start.14
  152.2 1.3 copy-start.3
  170.6 4.1 copy-start.1
  174.7 5.3 copy-start.7
  180.0 5.8 copy-start
  180.0 6.4 %copy-start.2 = (bf16[2,256,16,64]{3,2,1,0:T(8,128)(2,1)S(1)}, bf16[2,256,16,64]{3,2,1,0:T(8,128)(2,1)}, u32[]{:S(2)}) copy-start(bf16[2,256,16,64]{3,2,1,0:T(8,128)(2,1)} %reshape.82) | copy-start | bytes 3145732
  196.5 1.9 copy-start.13
  196.7 1.6 copy-start.10
  212.3 1.6 copy-start.4
  212.3 1.9 copy-start.15
  212.3 105.7 %reduce-scatter.7.cloned.1.call-start = ((), (), s32[]{:S(2)}) async-start(), calls=%async_computation.4 | async-start | bytes 2359296 | tf_op jit(solution)/shard_map/reduce_scatter | solution.py:61
  216.8 176.0 %reduce-scatter.9.cloned.1.call-start = ((), (), s32[]{:S(2)}) async-start(), calls=%async_computation.5 | async-start | bytes 9437184 | tf_op jit(solution)/shard_map/reduce_scatter | solution.py:61
  228.6 239.2 %reduce-scatter.11.cloned.1.call-start = ((), (), s32[]{:S(2)}) async-start(), calls=%async_computation.6 | async-start | bytes 9437184 | tf_op jit(solution)/shard_map/reduce_scatter | solution.py:61
  239.3 354.6 %all-reduce.4.cloned.1.call-start = ((), (), s32[]{:S(2)}) async-start(), calls=%async_computation.8 | async-start | bytes 6291456 | tf_op jit(solution)/shard_map/psum | solution.py:62
  513.1 9.8 %copy-start.12 = (f32[8,128]{1,0:T(8,128)}, f32[8,128]{1,0:T(8,128)S(1)}, u32[]{:S(2)}) copy-start(f32[8,128]{1,0:T(8,128)S(1)} %constant_dynamic-slice_fusion) | copy-start | bytes 12292
  593.9 2.9 copy-start.6
  593.9 4.5 copy-start.9
  596.8 3.0 copy-start.11
  596.8 3.8 copy-start.8
Sparse Core Ops, SparseCore 0:
  212.4 60.1 reduce-scatter.12
  276.8 41.1 reduce-scatter.6
  321.5 71.2 reduce-scatter.8
  396.5 71.2 reduce-scatter.10
  470.8 123.0 all-reduce.3

commit v3 on v2

--- a/solution.py
+++ b/solution.py
@@ -316,7 +316,7 @@
 def forward_kernel(
     lengths, tokens, cot, small, sh_q, sh_o, sh_u, sh_d,
     layer_out, wq_out, wo_out, wu_out, wd_out, qkv_out, slope_out, act_pair, first_pair, mixed_pair,
-    tok_pair, branch_pair, norm_out, inv_out, grad_out_ref, params_out, sums_out, act_out, mixed_out,
+    tok_pair, branch_pair, norm_out, inv_out, grad_out_ref, params_out, sums_out,
     x, wq, wo, wu, wd, qkv, mixed, norm, first_low, act, slope, acc, cot_v, gh2, out_v, gb, smalls, params,
     inv_v, sums, up_rows,
     ag_send, ag_recv, ag_local, sm_send, sm_recv, sm_local, io, pair_send, pair_recv, pair_local,
@@ -463,10 +463,6 @@
     lax.fori_loop(4, 8, up_step, 0)
     start_pair(3, act, act_pair, 512, range(2, 4))
     stores.append(pltpu.make_async_copy(slope, slope_out, io.at[8]))
-    stores[-1].start()
-    stores.append(pltpu.make_async_copy(act, act_out, io.at[14]))
-    stores[-1].start()
-    stores.append(pltpu.make_async_copy(mixed, mixed_out, io.at[15]))
     stores[-1].start()
     g_d.finish()
     g_d.local(ag_local.at[3]).wait()
@@ -539,8 +535,6 @@
         shape((rows, width), F32),
         shape((16, width), F32),
         shape((8, width), F32),
-        shape((rows, ff), BF16),
-        shape((rows, width), BF16),
     ]
     dma = pltpu.SemaphoreType.DMA
     scratch = [
@@ -571,7 +565,7 @@
         dma((7,)),
         dma((7,)),
         dma,
-        dma((16,)),
+        dma((14,)),
         dma((5, 4)),
         dma((5, 4)),
         dma((5, 4)),
@@ -594,6 +588,464 @@
     return jnp.concatenate([biases, gains, up_bias.reshape(4, 128), jnp.zeros((4, 128), BF16)], axis=0)
 
 
+BLOCKS = 12
+S1X, S1Y, S2X, S2Y, Z1, Z2, FM, FE, FF = range(9)
+
+
+class Reduce:
+    def __init__(self, place, prod, got_x, got_y, end_x, end_y, from_end, from_mid, out_at, send, recv, local):
+        self.p = place
+        self.prod, self.got_x, self.got_y, self.end_x, self.end_y = prod, got_x, got_y, end_x, end_y
+        self.from_end, self.from_mid, self.out_at = from_end, from_mid, out_at
+        self.send, self.recv, self.local = send, recv, local
+        z = place.z
+        self.mid = 1 + lax.div(z, 2)
+        self.end = 3 * lax.div(z, 2)
+        self.is_mid = z == self.mid
+        self.is_end = z == self.end
+        self.keep = pl.multiple_of(64 * (self.mid - 1), 64)
+        self.give = pl.multiple_of(64 * (2 - self.mid), 64)
+
+    def copy(self, kind, b, sending=True):
+        p = self.p
+        x, y, xn, yn = p.x, p.y, 1 - p.x, 1 - p.y
+        top, low_half = pl.ds(0, 64), pl.ds(64, 64)
+        if kind == S1X:
+            src, dst, dev = self.prod.at[b, :, xn, top], self.got_x.at[b], p.dev(f=p.fx)
+        elif kind == S1Y:
+            src, dst, dev = self.prod.at[b, yn, :, low_half], self.got_y.at[b], p.dev(f=p.fy)
+        elif kind == S2Y:
+            src, dst, dev = self.prod.at[b, yn, x, top], self.end_y.at[b], p.dev(f=p.fy)
+        elif kind == S2X:
+            src, dst, dev = self.prod.at[b, y, xn, low_half], self.end_x.at[b], p.dev(f=p.fx)
+        elif kind == Z1:
+            src, dst, dev = self.prod.at[b, y, x], self.from_end.at[b], p.dev(z=self.mid)
+        elif kind == Z2:
+            src, dst, dev = self.prod.at[b, y, x, pl.ds(self.give, 64)], self.from_mid.at[b], p.dev(z=3 - self.mid)
+        elif kind == FM:
+            lo = self.keep if sending else self.give
+            src, dst, dev = self.prod.at[b, y, x, pl.ds(self.keep, 64)], self.out_at(b, lo), p.dev(z=3 - self.mid)
+        elif kind == FE:
+            src, dst, dev = self.prod.at[b, y, x, pl.ds(self.keep, 64)], self.out_at(b, self.keep), p.dev(z=self.end)
+        else:
+            src, dst, dev = self.out_at(b, self.give), self.out_at(b, self.give), p.dev(z=self.end)
+        return remote(src, dst, self.send.at[kind, b], self.recv.at[kind, b], dev)
+
+    def begin(self, b):
+        self.copy(S1X, b).start()
+        self.copy(S1Y, b).start()
+
+    def second(self, b):
+        x, y = self.p.x, self.p.y
+        self.copy(S1X, b).wait_recv()
+        self.prod[b, :, x, 0:64] = self.prod[b, :, x, 0:64] + self.got_x[b]
+        self.copy(S2Y, b).start()
+        self.copy(S1Y, b).wait_recv()
+        self.prod[b, y, :, 64:128] = self.prod[b, y, :, 64:128] + self.got_y[b]
+        self.copy(S2X, b).start()
+
+    def along(self, b):
+        x, y = self.p.x, self.p.y
+        self.copy(S2Y, b).wait_recv()
+        self.copy(S2X, b).wait_recv()
+
+        @pl.when(self.is_end)
+        def _():
+            self.prod[b, y, x, 0:64] = self.prod[b, y, x, 0:64] + self.end_y[b]
+            self.prod[b, y, x, 64:128] = self.prod[b, y, x, 64:128] + self.end_x[b]
+            self.copy(Z1, b).start()
+
+        @pl.when(self.is_mid)
+        def _():
+            self.copy(Z1, b).wait_recv()
+            for lo, other in ((0, self.end_y), (64, self.end_x)):
+                total = self.prod[b, y, x, lo : lo + 64].astype(F32) + other[b].astype(F32)
+                total = total + self.from_end[b, lo : lo + 64].astype(F32)
+                self.prod[b, y, x, lo : lo + 64] = total.astype(BF16)
+            self.copy(Z2, b).start()
+
+    def write(self, b):
+        return pltpu.make_async_copy(
+            self.prod.at[b, self.p.y, self.p.x, pl.ds(self.keep, 64)], self.out_at(b, self.keep), self.local.at[b]
+        )
+
+    def hand_out(self, b):
+        x, y = self.p.x, self.p.y
+
+        @pl.when(self.is_mid)
+        def _():
+            self.copy(Z2, b).wait_recv()
+            here = pl.ds(self.keep, 64)
+            self.prod[b, y, x, here] = self.prod[b, y, x, here] + self.from_mid[b]
+            self.copy(FE, b).start()
+            self.copy(FM, b).start()
+            self.write(b).start()
+
+    def pass_on(self, b):
+        @pl.when(self.is_mid)
+        def _():
+            self.copy(FM, b, False).wait_recv()
+            self.copy(FF, b).start()
+
+    def tick(self, k):
+        for lag, step in enumerate((self.second, self.along, self.hand_out, self.pass_on)):
+            if 0 <= k - lag < BLOCKS:
+                step(k - lag)
+
+    def close(self, b):
+        for kind in (S1X, S1Y, S2X, S2Y):
+            self.copy(kind, b).wait_send()
+
+        @pl.when(self.is_end)
+        def _():
+            self.copy(Z1, b).wait_send()
+            self.copy(FE, b).wait_recv()
+            self.copy(FF, b).wait_recv()
+
+        @pl.when(self.is_mid)
+        def _():
+            for kind in (Z2, FM, FE, FF):
+                self.copy(kind, b).wait_send()
+            self.write(b).wait()
+
+
+def backward_kernel(
+    lengths, wq, wo, wu, wd, qkv, slope, act_pair, first_pair, mixed_pair, tok_pair, branch_pair,
+    norm_in, inv_in, gh2, params_in, sums_in,
+    token_grad, out_q, out_o, out_u, out_d, small_out,
+    lhs, wbuf, slope_v, branch, gi, gq, gm, gh, norm, inv, params, sums_v, upsum,
+    prod, got_x, got_y, end_x, end_y, from_end, from_mid,
+    s_send, s_got, s_total, s_all, s_out,
+    rs_send, rs_recv, rs_local, pair_send, pair_recv, load_sem, lhs_sem, w_sem, slope_sem,
+    sm_send, sm_recv, smz_send, smz_recv, store_sem,
+):
+    p = Place()
+    rows, width = gh.shape
+    slots = lengths.shape[0]
+    seq = rows // slots
+    planes = [lax.rem(p.f + k, 8) for k in range(1, 8)]
+    levels = [lax.rem(p.z + k, 4) for k in range(1, 4)]
+    barrier = pltpu.get_barrier_semaphore()
+    for g in planes:
+        pl.semaphore_signal(barrier, inc=1, device_id=p.dev(f=g), device_id_type=MESH)
+    for g in levels:
+        pl.semaphore_signal(barrier, inc=1, device_id=p.dev(z=g), device_id_type=MESH)
+
+    mine = pl.ds(pl.multiple_of(p.core * rows, rows), rows)
+
+    def lhs_copies(i):
+        if i < 4:
+            return [
+                pltpu.make_async_copy(
+                    act_pair.at[:, pl.ds(chip * 512 + i * 128, 128)],
+                    lhs.at[i % 2, :, pl.ds(chip * 128, 128)],
+                    lhs_sem.at[i, chip],
+                )
+                for chip in range(4)
+            ]
+        src = (first_pair, mixed_pair, tok_pair)[i - 4]
+        return [pltpu.make_async_copy(src, lhs.at[i % 2], lhs_sem.at[i, 0])]
+
+    def w_copy(i):
+        if i < 8:
+            j = i // 2
+            src = wu.at[:, pl.ds(j * 1024, 1024)] if i % 2 else wd.at[pl.ds(j * 1024, 1024)]
+        elif i == 8:
+            src = wo
+        else:
+            src = wq.at[:, pl.ds((i - 9) * 1024, 1024)]
+        return pltpu.make_async_copy(src, wbuf.at[i % 2], w_sem.at[i])
+
+    def slope_copy(j):
+        return pltpu.make_async_copy(slope.at[:, pl.ds(j * 1024, 1024)], slope_v.at[j % 2], slope_sem.at[j])
+
+    loads = [
+        pltpu.make_async_copy(src, dst, load_sem.at[i])
+        for i, (src, dst) in enumerate(
+            (
+                (branch_pair, branch), (gh2, gh), (qkv, gq.at[mine]), (norm_in, norm), (inv_in, inv),
+                (params_in, params), (sums_in, sums_v),
+            )
+        )
+    ]
+    for c in lhs_copies(0):
+        c.start()
+    loads[0].start()
+    for c in lhs_copies(1):
+        c.start()
+    w_copy(0).start()
+    slope_copy(0).start()
+    for c in loads[1:]:
+        c.start()
+
+    def out_at(b, lo):
+        if b < 4:
+            return out_d.at[pl.ds(pl.multiple_of(128 * b + lo, 16), 64)]
+        if b < 8:
+            return out_u.at[pl.ds(lo, 64), pl.ds((b - 4) * 1024, 1024)]
+        if b == 8:
+            return out_o.at[pl.ds(lo, 64)]
+        return out_q.at[pl.ds(lo, 64), pl.ds((b - 9) * 1024, 1024)]
+
+    red = Reduce(p, prod, got_x, got_y, end_x, end_y, from_end, from_mid, out_at, rs_send, rs_recv, rs_local)
+
+    def produce(b, left, right):
+        prod[b] = dot_tn(left, right).astype(BF16).reshape(2, 2, 128, 1024)
+        red.begin(b)
+
+    def to_pair(index, ref, cols):
+        here = ref.at[mine, cols]
+        return remote(here, here, pair_send.at[index], pair_recv.at[index], p.dev(f=p.fs))
+
+    pl.semaphore_wait(barrier, 10)
+    loads[0].wait()
+    for b in range(4):
+        for c in lhs_copies(b):
+            c.wait()
+        produce(b, lhs[b % 2], branch[...])
+        for c in lhs_copies(b + 2) if b < 4 else ():
+            c.start()
+    loads[1].wait()
+
+    def block_cols(j):
+        return pl.ds(j * 1024, 1024)
+
+    def up_block(j):
+        to_pair(j, gi, block_cols(j)).wait_recv()
+        produce(4 + j, lhs[0], gi[:, j * 1024 : (j + 1) * 1024])
+
+    for j in range(4):
+        w_copy(2 * j).wait()
+        w_copy(2 * j + 1).start()
+        slope_copy(j).wait()
+        if j < 3:
+            slope_copy(j + 1).start()
+        inner = (dot_nt(branch[mine], wbuf[0]) * slope_v[j % 2].astype(F32)).astype(BF16)
+        gi[mine, j * 1024 : (j + 1) * 1024] = inner
+        to_pair(j, gi, block_cols(j)).start()
+        upsum[j : j + 1] = jnp.sum(inner.astype(F32), axis=0, keepdims=True)
+        w_copy(2 * j + 1).wait()
+        w_copy(2 * j + 2).start()
+        gh[...] += dot_nt(gi[mine, j * 1024 : (j + 1) * 1024], wbuf[1])
+        if j == 0:
+            for c in lhs_copies(4):
+                c.wait()
+        if j > 0:
+            up_block(j - 1)
+            red.tick(j - 1)
+    for c in loads[2:]:
+        c.wait()
+    ga = branch
+    e = gh[...]
+    scaled = e * params[6:7]
+    n = norm[...]
+    sums_v[3:4] = jnp.sum(e, axis=0, keepdims=True)
+    sums_v[4:5] = jnp.sum(e * n, axis=0, keepdims=True)
+    gh[...] = inv[:, 0:1] * (scaled - row_mean(scaled) - n * row_mean(scaled * n))
+    ga[mine] = gh[...].astype(BF16)
+    whole = pl.ds(0, 1024)
+    to_pair(4, ga, whole).start()
+    sums_v[5:6] = jnp.sum(ga[mine].astype(F32), axis=0, keepdims=True)
+    up_block(3)
+    for c in lhs_copies(6):
+        c.start()
+    w_copy(8).wait()
+    w_copy(9).start()
+    gm[...] = dot_nt(ga[mine], wbuf[0]).astype(BF16)
+    w_copy(10).start()
+    for c in lhs_copies(5):
+        c.wait()
+    to_pair(4, ga, whole).wait_recv()
+    produce(8, lhs[1], ga[...])
+    red.tick(3)
+
+    left = lax.broadcasted_iota(jnp.int32, (seq, 128), 1) < HEAD_SIZE
+    key_row = lax.broadcasted_iota(jnp.int32, (seq, seq), 0)
+    scale = 1.0 / math.sqrt(HEAD_SIZE)
+
+    def attend(step, carry):
+        slot, pair_of = lax.rem(step, slots), lax.div(step, slots)
+        at_rows = pl.ds(pl.multiple_of(slot * seq, seq), seq)
+        own_rows = pl.ds(pl.multiple_of(p.core * rows + slot * seq, seq), seq)
+        col = pl.multiple_of(pair_of * 128, 128)
+        at_q = pl.ds(col, 128)
+        at_k = pl.ds(pl.multiple_of(width + col, 128), 128)
+        at_v = pl.ds(pl.multiple_of(2 * width + col, 128), 128)
+        q, k, v = gq[own_rows, at_q], gq[own_rows, at_k], gq[own_rows, at_v]
+        do = gm[at_rows, at_q]
+        dead = key_row >= lengths[slot]
+        parts = []
+        for head in range(2):
+            lanes = left if head == 0 else ~left
+            k_head = jnp.where(lanes, k, jnp.zeros_like(k))
+            v_head = jnp.where(lanes, v, jnp.zeros_like(v))
+            scores = jnp.where(dead, -1e30, dot_nt(k_head, q) * scale)
+            exps = jnp.exp(scores - jnp.max(scores, axis=0, keepdims=True))
+            probs = exps * (1.0 / jnp.sum(exps, axis=0, keepdims=True))
+            d_probs = dot_nt(v_head, do)
+            shared = jnp.sum(probs * d_probs, axis=0, keepdims=True)
+            d_scores = (probs * (d_probs - shared)).astype(BF16)
+            parts.append(
+                (dot_tn(d_scores, k) * scale, dot_nn(d_scores, q) * scale, dot_nn(probs.astype(BF16), do))
+            )
+        for at, one, two in zip((at_q, at_k, at_v), *parts):
+            gq[own_rows, at] = jnp.where(left, one, two).astype(BF16)
+        return carry
+
+    steps = 8 * slots
+    for quarter in range(4):
+        lax.fori_loop(quarter * steps // 4, (quarter + 1) * steps // 4, attend, 0)
+        if quarter % 2:
+            for j in range(3):
+                to_pair(5 + 3 * (quarter // 2) + j, gq, pl.ds(j * 1024 + 512 * (quarter // 2), 512)).start()
+        red.tick(4 + quarter)
+    for c in lhs_copies(6):
+        c.wait()
+    for j in range(3):
+        for half in range(2):
+            to_pair(5 + 3 * half + j, gq, pl.ds(j * 1024 + 512 * half, 512)).wait_recv()
+        produce(9 + j, lhs[0], gq[:, j * 1024 : (j + 1) * 1024])
+    sums_v[6:7] = jnp.sum(gq[mine, 0:1024].astype(F32), axis=0, keepdims=True)
+    sums_v[7:8] = jnp.sum(gq[mine, 2048:3072].astype(F32), axis=0, keepdims=True)
+
+    order = (6, 7, 5, 3, 2, 1, 4, 0)
+    for g in range(8):
+        cols = slice(g * 128, (g + 1) * 128)
+        for i, row in enumerate(order):
+            s_send[g, i : i + 1] = sums_v[row : row + 1, cols]
+        for i in range(4):
+            lo = (g % 2) * 512 + i * 128
+            s_send[g, 8 + i : 9 + i] = upsum[g // 2 : g // 2 + 1, lo : lo + 128]
+
+    def small_to(k):
+        g = planes[k]
+        return remote(s_send.at[g], s_got.at[p.f], sm_send.at[k], sm_recv.at[k], p.dev(f=g))
+
+    def small_from(k):
+        g = lax.rem(p.f + 7 - k, 8)
+        return remote(s_send.at[g], s_got.at[g], sm_send.at[k], sm_recv.at[k], p.dev(f=g))
+
+    def level_to(k):
+        return remote(s_total, s_all.at[p.z], smz_send.at[k], smz_recv.at[k], p.dev(z=levels[k]))
+
+    def level_from(k):
+        g = lax.rem(p.z + 3 - k, 4)
+        return remote(s_total, s_all.at[g], smz_send.at[k], smz_recv.at[k], p.dev(z=g))
+
+    for k in range(7):
+        small_to(k).start()
+    s_got[p.f] = s_send[p.f]
+
+    for j in range(3):
+        w_copy(9 + j).wait()
+        gh[...] += dot_nt(gq[mine, j * 1024 : (j + 1) * 1024], wbuf[(9 + j) % 2])
+        if j == 0:
+            w_copy(11).start()
+    store = pltpu.make_async_copy(gh, token_grad, store_sem.at[0])
+    store.start()
+    red.tick(8)
+    for k in range(7):
+        small_from(k).wait_recv()
+    total = s_got[0]
+    for g in range(1, 8):
+        total = total + s_got[g]
+    s_total[...] = total
+    for k in range(3):
+        level_to(k).start()
+    s_all[p.z] = total
+    for k in range(9, BLOCKS + 3):
+        red.tick(k)
+    for k in range(3):
+        level_from(k).wait_recv()
+    s_out[...] = (s_all[0] + s_all[1]) + (s_all[2] + s_all[3])
+    small_store = pltpu.make_async_copy(s_out, small_out, store_sem.at[1])
+    small_store.start()
+    for b in range(BLOCKS):
+        red.close(b)
+    for k in range(7):
+        small_to(k).wait_send()
+    for k in range(3):
+        level_to(k).wait_send()
+    for j in range(4):
+        to_pair(j, gi, block_cols(j)).wait_send()
+    to_pair(4, ga, whole).wait_send()
+    for j in range(3):
+        for half in range(2):
+            to_pair(5 + 3 * half + j, gq, pl.ds(j * 1024 + 512 * half, 512)).wait_send()
+    store.wait()
+    small_store.wait()
+
+
+def backward_call(lengths, saved):
+    wq, wo, wu, wd, qkv, slope = saved[:6]
+    rows, width = qkv.shape[0], wo.shape[0]
+    ff = wu.shape[1]
+    anyspace = pl.BlockSpec(memory_space=pl.ANY)
+    shape = jax.ShapeDtypeStruct
+    dma = pltpu.SemaphoreType.DMA
+    outs = [
+        shape((rows, width), F32),
+        shape((width // 8, 3 * width), BF16),
+        shape((width // 8, width), BF16),
+        shape((width // 8, ff), BF16),
+        shape((ff // 8, width), BF16),
+        shape((16, 128), F32),
+    ]
+    scratch = [
+        pltpu.VMEM((2, 2 * rows, 512), BF16),
+        pltpu.VMEM((2, 1024, 1024), BF16),
+        pltpu.VMEM((2, rows, 1024), BF16),
+        pltpu.VMEM((2 * rows, width), BF16),
+        pltpu.VMEM((2 * rows, ff), BF16),
+        pltpu.VMEM((2 * rows, 3 * width), BF16),
+        pltpu.VMEM((rows, width), BF16),
+        pltpu.VMEM((rows, width), F32),
+        pltpu.VMEM((rows, width), F32),
+        pltpu.VMEM((rows, 128), F32),
+        pltpu.VMEM((16, width), F32),
+        pltpu.VMEM((8, width), F32),
+        pltpu.VMEM((4, width), F32),
+        pltpu.VMEM((BLOCKS, 2, 2, 128, 1024), BF16),
+        pltpu.VMEM((BLOCKS, 2, 64, 1024), BF16),
+        pltpu.VMEM((BLOCKS, 2, 64, 1024), BF16),
+        pltpu.VMEM((BLOCKS, 64, 1024), BF16),
+        pltpu.VMEM((BLOCKS, 64, 1024), BF16),
+        pltpu.VMEM((BLOCKS, 128, 1024), BF16),
+        pltpu.VMEM((BLOCKS, 64, 1024), BF16),
+        pltpu.VMEM((8, 16, 128), F32),
+        pltpu.VMEM((8, 16, 128), F32),
+        pltpu.VMEM((16, 128), F32),
+        pltpu.VMEM((4, 16, 128), F32),
+        pltpu.VMEM((16, 128), F32),
+        dma((9, BLOCKS)),
+        dma((9, BLOCKS)),
+        dma((BLOCKS,)),
+        dma((11,)),
+        dma((11,)),
+        dma((7,)),
+        dma((7, 4)),
+        dma((12,)),
+        dma((4,)),
+        dma((7,)),
+        dma((7,)),
+        dma((3,)),
+        dma((3,)),
+        dma((2,)),
+    ]
+    return pl.pallas_call(
+        backward_kernel,
+        out_shape=outs,
+        in_specs=[pl.BlockSpec(memory_space=pltpu.SMEM)] + [anyspace] * len(saved),
+        out_specs=[anyspace] * len(outs),
+        scratch_shapes=scratch,
+        name="backward",
+        cost_estimate=pl.CostEstimate(flops=4 * 512 * 12582912, bytes_accessed=60 * MIB, transcendentals=4 * MIB),
+        compiler_params=pltpu.CompilerParams(
+            collective_id=1, has_side_effects=True, vmem_limit_bytes=60 * MIB
+        ),
+    )(lengths, *saved)
+
+
 def plane(
     tokens,
     lengths,
@@ -606,91 +1058,18 @@
     up_bias,
     gains,
 ):
-    slots = lengths.shape[0]
-    rows, width = tokens.shape
-    seq = rows // slots
-    heads = width // HEAD_SIZE
-    scale = 1.0 / math.sqrt(HEAD_SIZE)
-    got = forward_call(
-        tokens, lengths, cotangent, qkv_weight, out_weight, up_weight, down_weight,
-        pack_small(biases, up_bias, gains),
-    )
-    layer_out, w_qkv, w_out, w_up, w_down, qkv, slope = got[:7]
-    grad_branch_pair, first, first_inverse, grad_h2, params, sums, act_low, mixed = got[11:]
-    first_inverse = first_inverse[:, :1]
-    gain_one = params[6]
-    first_low = low(first * gain_one + params[3])
-    grad_branch = low(grad_h2)
-
-    def split(values):
-        return values.reshape(slots, seq, heads, HEAD_SIZE)
-
-    def join(values):
-        return values.reshape(rows, width)
-
-    query, key, value = (split(qkv[:, j * width : (j + 1) * width]) for j in range(3))
-    live = jnp.arange(seq)[None, :] < lengths[:, None]
-    scores = scale * jnp.einsum(
-        "bshd,bthd->bhst", query, key, preferred_element_type=jnp.float32
-    )
-    scores = jnp.where(live[:, None, None, :], scores, -1e30)
-    exps = jnp.exp(scores - jnp.max(scores, axis=-1, keepdims=True))
-    probs = exps / jnp.sum(exps, axis=-1, keepdims=True)
-    probs_low = low(probs)
-    down_grad = reduce_weight(transposed_left(act_low, grad_branch))
-    grad_inner = low(transposed_right(grad_branch, w_down) * slope)
-    up_grad = reduce_weight(transposed_left(first_low, grad_inner))
-    grad_first = grad_h2 + transposed_right(grad_inner, w_up)
-    grad_h1 = norm_back(grad_first, first, first_inverse, gain_one)
-    grad_attn = low(grad_h1)
-    out_grad = reduce_weight(transposed_left(mixed, grad_attn))
-    grad_mixed = split(low(transposed_right(grad_attn, w_out)))
-    grad_probs = jnp.einsum(
-        "bshd,bthd->bhst", grad_mixed, value, preferred_element_type=jnp.float32
-    )
-    shared = jnp.sum(probs * grad_probs, axis=-1, keepdims=True)
-    grad_scores = low(probs * (grad_probs - shared))
-    grad_query = scale * jnp.einsum(
-        "bhst,bthd->bshd", grad_scores, key, preferred_element_type=jnp.float32
-    )
-    grad_key = scale * jnp.einsum(
-        "bhst,bshd->bthd", grad_scores, query, preferred_element_type=jnp.float32
-    )
-    grad_value = jnp.einsum(
-        "bhst,bshd->bthd", probs_low, grad_mixed, preferred_element_type=jnp.float32
-    )
-    grad_qkv = jnp.concatenate(
-        [join(low(grad_query)), join(low(grad_key)), join(low(grad_value))], axis=1
-    )
-    qkv_grad = reduce_weight(transposed_left(tokens, grad_qkv))
-    token_grad = grad_h1 + transposed_right(grad_qkv, w_qkv)
-    small = jnp.stack(
-        [
-            column_sum(grad_qkv[:, :width]),
-            column_sum(grad_qkv[:, 2 * width :]),
-            column_sum(grad_attn),
-            column_sum(grad_first),
-            sums[2],
-            sums[1],
-            column_sum(grad_first * first),
-            sums[0],
-        ]
-    )
-    owner = lax.axis_index("fsdp")
-    small, up_sum = lax.psum((small, column_sum(grad_inner)), ("fsdp", "rep"))
-    own, own_up = biases.shape[1], up_bias.shape[0]
-    small = lax.dynamic_slice(small, (0, owner * own), (8, own))
-    up_bias_grad = lax.dynamic_slice(up_sum, (owner * own_up,), (own_up,))
+    small_in = pack_small(biases, up_bias, gains)
+    layer_out, *saved = forward_call(
+        tokens, lengths, cotangent, qkv_weight, out_weight, up_weight, down_weight, small_in
+    )
+    token_grad, *weight_grads, small = backward_call(lengths, saved)
     return (
         layer_out,
         token_grad,
-        qkv_grad,
-        out_grad,
-        up_grad,
-        down_grad,
+        *(grad.astype(F32) for grad in weight_grads),
         small[:6],
-        up_bias_grad,
-        small[6:],
+        small[8:12].reshape(-1),
+        small[6:8],
     )
 
 

time: 615 us -> 297 us (0.48)
  waiting for transfers between devices: 297 us -> 0 us
  Pallas kernels: 121 us -> 275 us
  matrix products: 73.4 us -> 0 us
  blocking collectives: 44.2 us -> 0 us
  local copies, waits for them, and re-layouts: 47.8 us -> 6.67 us
  between operations: 14.6 us -> 0.91 us
    reduce_scatter x3 -> x0, waiting for transfers between devices: 193 us -> none  [reduce_weight(): shard = lax.psum_scatter(low(grad), 'fsdp', scatter_dimension=0, tiled=True)]
    pallas_call x0 -> x1, Pallas kernels: none -> 154 us  [backward_call(): pl.pallas_call(backward_kernel, out_shape=outs, in_specs=[pl.BlockSpec(me...]
    psum x1 -> x0, waiting for transfers between devices: 71.1 us -> none  [reduce_weight(): return lax.psum(shard, 'rep').astype(jnp.float32)]
    dot_general x12 -> x0, matrix products: 68.1 us -> none  [the longest x4 30.1 us: transposed_left(): lax.dot_general(left_side, right_side, (((0,), (0,)), ((), ())), preferre...]
    psum x1 -> x0, blocking collectives: 44.2 us -> none  [plane(): small, up_sum = lax.psum((small, column_sum(grad_inner)), ('fsdp', 'rep'))]
    unnamed x6 -> x0, waiting for transfers between devices: 33.3 us -> none
    unnamed x45 -> x10, local copies, waits for them, and re-layouts: 20.3 us -> 2.72 us
    reshape x7 -> x1, local copies, waits for them, and re-layouts: 16.4 us -> 1.26 us  [plane(): small[8:12].reshape(-1)]
  transfers between devices with their start and end apart: 5 -> 0, of which waited for: 5 -> 0; matrix products, arithmetic and copies ran while one was open for 6% -> 0% of each run, Pallas kernels for 0% -> 0%
where the time goes in v3:
time: 297 us; the launch traced here: 291 us
  Pallas kernels  275 us (93%)
  other arithmetic  8.69 us (3%)
  local copies, waits for them, and re-layouts  6.67 us (2%)
    pallas_call x1, Pallas kernels, backward_call(): pl.pallas_call(backward_kernel, out_shape=outs, in_specs=[pl.BlockSpec(me...  154 us
    pallas_call x1, Pallas kernels, forward_call(): pl.pallas_call(forward_kernel, out_shape=outs, in_specs=[pl.BlockSpec(mem...  121 us
    convert_element_type x4, other arithmetic, plane(): grad.astype(F32)  7.31 us

profile of v3, /device:TPU:0, one launch (start us, length us, event | category | flops | bytes accessed | tf_op | source)
XLA Modules:
  0.0 290.9 jit_solution(15081391634306244045)
XLA Ops:
  0.7 0.1 pad.3.clone
  0.7 1.4 maximum_maximum_fusion.small
  2.1 121.1 %forward.1 = (bf16[512,1024]{1,0:T(8,128)(2,1)}, bf16[1024,3072]{1,0:T(8,128)(2,1)}, bf16[1024,1024]{1,0:T(8,128)(2,1)}, bf16[1024,4096]{1,0:T(8,128)(2,1)}, bf1...) custom-call(s32[2]{0:T(128)} %lengths.3, ...), custom_call_target="tpu_custom_call" | custom-call | flops 12884901888 | bytes 62914560 | tf_op jit(solution)/shard_map/forward/pallas_call | solution.py:573
  123.2 153.5 %backward.1 = (f32[512,1024]{1,0:T(8,128)}, bf16[128,3072]{1,0:T(8,128)(2,1)}, bf16[128,1024]{1,0:T(8,128)(2,1)}, bf16[128,4096]{1,0:T(8,128)(2,1)}, bf16[512,1024]{1,0:T(8,128)(2,1)}, /*index=5*/f32[16,128]{1,0:T(8,128)}) custom-call(s32[2]{0:T(128)} %lengths.3, bf16[1024,3072]{1,0:T(8,128)(2,1)} %get-tuple-element.33.wq, ...), custom_call_target="tpu_custom_call" | custom-call | flops 25769803776 | bytes 62914560 | tf_op jit(solution)/shard_map/backward/pallas_call | solution.py:1035
  276.7 0.0 copy-start.2
  276.7 1.3 slice.11
  278.1 1.3 slice_bitcast_fusion
  279.3 1.3 slice.9
  280.6 1.8 convert_element_type.13
  282.4 2.4 convert_element_type.12
  284.8 0.0 copy-done.2
  284.8 0.0 copy-start.1
  284.8 1.5 convert_element_type.14
  286.4 0.0 copy-done.1
  286.4 0.0 copy-start.3
  286.4 0.0 copy-start
  286.4 1.6 convert_element_type.15
  287.9 0.0 copy-done.3
  287.9 1.0 copy.21
  288.9 0.4 copy-done
  289.3 1.3 copy.22
  (1 shorter events, 0.0 us)
Async XLA Ops:
  276.7 8.1 %copy-start.2 = (bf16[128,4096]{1,0:T(8,128)(2,1)S(1)}, bf16[128,4096]{1,0:T(8,128)(2,1)}, u32[]{:S(2)}) copy-start(bf16[128,4096]{1,0:T(8,128)(2,1)} %get-tuple-element.52) | copy-start | bytes 3145732
  284.8 1.5 copy-start.1
  286.4 1.6 copy-start.3
  286.4 3.0 %copy-start = (f32[512,1024]{1,0:T(8,128)S(1)}, f32[512,1024]{1,0:T(8,128)}, u32[]{:S(2)}) copy-start(f32[512,1024]{1,0:T(8,128)} %get-tuple-element.65) | copy-start | bytes 6291460
